TPU v7x, 32 devices: a whole 2x2x4 slice. The times are simulated.
32 devices in a mesh: dp: 8 (over z, x), fsdp: 4 (over y, core).
Axes of the slice: x: 2, y: 2, z: 4, core: 2. Of those that a mesh axis runs over, the one named last changes fastest.
Arguments:
- tokens: bfloat16 [32, 1024, 768], P(('dp', 'fsdp')), may hold values from -11 to 11
- lengths: int32 [32], P(('dp', 'fsdp')), may hold values from 256 to 1024, as said below
- buckets: int32 [2047], replicated, may hold values from 0 to 31
- rel_table: float32 [32, 12], replicated, may hold values from -4 to 4
- gain_attn: float32 [768], replicated, may hold values from 0.5 to 1.5
- gain_ff: float32 [768], replicated, may hold values from 0.5 to 1.5
- w_qkv: bfloat16 [768, 2304], replicated, may hold values from -0.21875 to 0.21875
- w_out: bfloat16 [768, 768], replicated, may hold values from -0.875 to 0.875
- w_in: bfloat16 [768, 3072], replicated, may hold values from -0.21875 to 0.21875
- w_down: bfloat16 [3072, 768], replicated, may hold values from -0.109375 to 0.109375
- adapters: bfloat16 [622080], P(('dp', 'fsdp')), may hold values from -5 to 5
- cotangent: bfloat16 [32, 1024, 768], P(('dp', 'fsdp')), may hold values from -6 to 6
Outputs:
- block_out: bfloat16 [32, 1024, 768], P(('dp', 'fsdp'))
- tokens_grad: float32 [32, 1024, 768], P(('dp', 'fsdp'))
- adapters_grad: float32 [622080], P(('dp', 'fsdp'))
- root_squares: float32 [4], replicated
Inputs may be any that keep to these rules, and one draw needn't show every extreme that they name: `lengths`: each sequence's count of valid leading positions; in every draw one sequence has all 1024.
All inputs are finite; a program needn't handle non-finite values.
Results may differ from a plain program's by a relative error of at most 0.017.
Values may be sent and summed in bfloat16 or wider, within the bound.
A program may use at most 512 MiB of HBM per device.

v0:
```python
import functools

import jax
import jax.numpy as jnp
from jax import lax
from jax.experimental import pallas as pl
from jax.experimental.pallas import tpu as pltpu
from jax.sharding import PartitionSpec as P

D = 768
FF = 3072
HEADS = 12
HDIM = 64
EXPERTS = 10
RANK = 4
FANS = ((D, D), (D, D), (D, D), (D, D), (D, FF), (FF, D))
COLS = EXPERTS * RANK
LANES = 128

EPSILON = 1e-06
MASKED = -1000000000.0
GELU_SCALE = 0.7978845608028654
GELU_CUBIC = 0.044715
LOG2E = 1.4426950408889634
LN2 = 0.6931471805599453
QUERY_SCALE = 0.125 * LOG2E

ROWS = 256
MIDDLE_ROWS = 512
CHUNK = 512
QBLOCK = 256
UP_ROWS = 48
DOWN_ROWS = 2 * COLS
VMEM_BYTES = 60 * 1024 * 1024

F32 = jnp.float32
BF16 = jnp.bfloat16


def dot(a, b):
    return lax.dot_general(a, b, (((1,), (0,)), ((), ())), preferred_element_type=F32)


def dot_nt(a, b):
    return lax.dot_general(a, b, (((1,), (1,)), ((), ())), preferred_element_type=F32)


def dot_tn(a, b):
    return lax.dot_general(a, b, (((0,), (0,)), ((), ())), preferred_element_type=F32)


def lane_iota(shape):
    return lax.broadcasted_iota(jnp.int32, shape, 1)


def row_iota(shape):
    return lax.broadcasted_iota(jnp.int32, shape, 0)


def gates_of(logits):
    weights = jnp.exp(logits - jnp.max(logits, axis=0, keepdims=True))
    return weights * (4.0 / jnp.sum(weights, axis=0, keepdims=True))


def gate_grads(grad_mixed, lowrank, gates):
    product = grad_mixed * lowrank
    summed = product
    for step in range(1, RANK):
        summed = summed + pltpu.roll(product, COLS - step, 0)
    centre = jnp.sum(gates * product, axis=0, keepdims=True)
    first = row_iota(gates.shape) % RANK == 0
    return grad_mixed * gates, jnp.where(first, gates * (summed - centre), 0.0)


def pad_rows(value, rows):
    return jnp.concatenate([value, jnp.zeros((rows - value.shape[0], value.shape[1]), F32)], axis=0)


def single_gates(packed):
    turned = packed.T
    lowrank = turned[:COLS]
    gates = gates_of(turned[COLS : 2 * COLS])
    mixed = pad_rows(lowrank * gates, LANES).astype(BF16)
    return lowrank, gates, mixed, mixed.T


def single_deltas(grad_mixed, lowrank, gates):
    parts = gate_grads(grad_mixed.T[:COLS], lowrank, gates)
    delta = pad_rows(jnp.concatenate(parts, axis=0), LANES).astype(BF16)
    return delta, delta.T


def rms_inverse(values):
    return lax.rsqrt(jnp.mean(values * values, axis=-1, keepdims=True) + EPSILON)


def rms_backward(values, gain, inverse, grad_normed):
    weighted = grad_normed * gain
    return inverse * weighted - values * (
        inverse * inverse * inverse * jnp.mean(values * weighted, axis=-1, keepdims=True)
    )


def params(**more):
    return pltpu.CompilerParams(vmem_limit_bytes=VMEM_BYTES, **more)


def whole(shape):
    zeros = (0,) * len(shape)
    return pl.BlockSpec(shape, lambda *_: zeros, pipeline_mode=pl.Buffered(1))


def project_kernel(
    x_ref, gain_ref, w_ref, ar_ref, b_ref, qt_ref, k_ref, kt_ref, v_ref, vt_ref, zg_ref
):
    values = x_ref[...].astype(F32)
    normed = (values * rms_inverse(values) * gain_ref[...]).astype(BF16)
    packed = dot(normed, ar_ref[...]).T
    lowrank = packed[: 3 * COLS]
    gates = jnp.concatenate(
        [gates_of(packed[first : first + COLS]) for first in range(3 * COLS, 6 * COLS, COLS)], axis=0
    )
    zg_ref[: 3 * COLS] = lowrank
    zg_ref[3 * COLS :] = gates
    mixed = pad_rows(lowrank * gates, LANES).astype(BF16).T
    for index in range(3):
        columns = slice(index * D, (index + 1) * D)
        part = dot(normed, w_ref[:, columns]) + dot(mixed, b_ref[:, columns])
        if index == 0:
            qt_ref[...] = (part * QUERY_SCALE).astype(BF16).T
        else:
            low = part.astype(BF16)
            natural, turned = ((k_ref, kt_ref), (v_ref, vt_ref))[index - 1]
            natural[...] = low
            turned[...] = low.T


def project(x, gain, w_qkv, ar_qkv, b_qkv):
    length = x.shape[0]
    tile = pl.BlockSpec((ROWS, D), lambda i: (i, 0))
    turned = pl.BlockSpec((D, ROWS), lambda i: (0, i))
    natural_shape = jax.ShapeDtypeStruct((length, D), BF16)
    turned_shape = jax.ShapeDtypeStruct((D, length), BF16)
    return pl.pallas_call(
        project_kernel,
        grid=(length // ROWS,),
        in_specs=[
            tile,
            whole((1, D)),
            whole(w_qkv.shape),
            whole(ar_qkv.shape),
            whole(b_qkv.shape),
        ],
        out_specs=[
            turned,
            tile,
            turned,
            tile,
            turned,
            pl.BlockSpec((6 * COLS, ROWS), lambda i: (0, i)),
        ],
        out_shape=[
            turned_shape,
            natural_shape,
            turned_shape,
            natural_shape,
            turned_shape,
            jax.ShapeDtypeStruct((6 * COLS, length), F32),
        ],
        compiler_params=params(),
        name="project",
    )(x, gain, w_qkv, ar_qkv, b_qkv)


def bias_table(offset_row, length):
    spread = jnp.broadcast_to(offset_row, (LANES, 2 * length))
    return pltpu.roll(spread, 2 * length - (LANES - 1), 1, stride=1, stride_axis=0)


def add_bias(scores, table_ref, start, length):
    width = scores.shape[1]
    parts = []
    for block in range(length // LANES):
        offset = start - LANES * block + (length - LANES)
        parts.append(
            scores[block * LANES : (block + 1) * LANES] + table_ref[:, offset : offset + width]
        )
    return jnp.concatenate(parts, axis=0)


def key_extras(length_ref, shape, odd):
    lane = lane_iota(shape) - (0 if odd else HDIM)
    invalid = row_iota(shape) >= length_ref[0]
    extras = jnp.where((lane == 0) & invalid, MASKED, 0.0)
    return jnp.where((lane >= 1) & (lane <= 3), 1.0, extras).astype(BF16)


def head_lanes(odd):
    lane = lane_iota((1, LANES))
    return ((lane >= HDIM) if odd else (lane < HDIM)).astype(F32).astype(BF16)


def extra_rows(rows):
    width = rows[0].shape[1]
    index = row_iota((8, width))
    block = jnp.zeros((8, width), F32)
    for place, row in enumerate(rows):
        block = jnp.where(index == place, row, block)
    return jnp.concatenate([block, jnp.zeros((HDIM - 8, width), F32)], axis=0).astype(BF16)


def split_three(row):
    high = row.astype(BF16).astype(F32)
    middle = (row - high).astype(BF16).astype(F32)
    return high, middle, row - high - middle


def join_rows(rows, extras, odd):
    return jnp.concatenate([extras, rows] if odd else [rows, extras], axis=0)


def attend_kernel(length_ref, off_ref, qt_ref, k_ref, vt_ref, o_ref, lse_ref, table, key_more):
    length = k_ref.shape[0]

    @pl.when(pl.program_id(0) == 0)
    def _():
        for odd in range(2):
            key_more[odd] = key_extras(length_ref, k_ref.shape, odd)

    for odd in range(2):
        half = slice(odd * HDIM, (odd + 1) * HDIM)
        table[odd] = bias_table(off_ref[0, odd : odd + 1, :], length)
        keys = k_ref[...] * head_lanes(odd) + key_more[odd]
        ones = jnp.ones((1, length), F32)
        queries = join_rows(qt_ref[half, :], extra_rows([ones]), odd)
        values = jnp.concatenate([vt_ref[half, :], jnp.ones((16, length), BF16)], axis=0)
        starts = range(0, length, QBLOCK)
        scores = [
            add_bias(dot(keys, queries[:, start : start + QBLOCK]), table.at[odd], start, length)
            for start in starts
        ]
        peaks = [jnp.max(part, axis=0, keepdims=True) for part in scores]
        weights = [jnp.exp2(part - peak).astype(BF16) for part, peak in zip(scores, peaks)]
        for start, peak, part in zip(starts, peaks, weights):
            columns = slice(start, start + QBLOCK)
            summed = dot(values, part)
            total = summed[HDIM : HDIM + 1]
            o_ref[half, columns] = (summed[:HDIM] / total).astype(BF16)
            lse_ref[0, odd : odd + 1, columns] = peak + jnp.log2(total)


def attend(length_valid, offsets, qt, k, vt):
    length = k.shape[0]
    turned = pl.BlockSpec((LANES, length), lambda p: (p, 0))
    natural = pl.BlockSpec((length, LANES), lambda p: (0, p))
    pair_rows = pl.BlockSpec((1, 2, 2 * length), lambda p: (p, 0, 0))
    return pl.pallas_call(
        attend_kernel,
        grid=(HEADS // 2,),
        in_specs=[
            pl.BlockSpec(memory_space=pltpu.SMEM),
            pair_rows,
            turned,
            natural,
            turned,
        ],
        out_specs=[turned, pl.BlockSpec((1, 2, length), lambda p: (p, 0, 0))],
        out_shape=[
            jax.ShapeDtypeStruct((D, length), BF16),
            jax.ShapeDtypeStruct((HEADS // 2, 2, length), F32),
        ],
        scratch_shapes=[
            pltpu.VMEM((2, LANES, 2 * length), F32),
            pltpu.VMEM((2, length, LANES), BF16),
        ],
        compiler_params=params(),
        name="attend",
    )(length_valid, offsets, qt, k, vt)


def attend_back_kernel(
    length_ref,
    off_ref,
    qt_ref,
    k_ref,
    kt_ref,
    v_ref,
    ot_ref,
    gt_ref,
    lse_ref,
    dq_ref,
    dk_ref,
    dv_ref,
    table,
    key_more,
    weights_all,
    grads_all,
):
    length = k_ref.shape[0]

    @pl.when(pl.program_id(0) == 0)
    def _():
        for odd in range(2):
            key_more[odd] = key_extras(length_ref, k_ref.shape, odd)

    lane = lane_iota((1, LANES))
    first_lanes = lane < HDIM
    grad_query_parts = []
    for odd in range(2):
        half = slice(odd * HDIM, (odd + 1) * HDIM)
        table[odd] = bias_table(off_ref[0, odd : odd + 1, :], length)
        keys = k_ref[...] * head_lanes(odd) + key_more[odd]
        place = lane - (0 if odd else HDIM)
        value_more = ((place >= 0) & (place < 3)).astype(F32).astype(BF16)
        values = v_ref[...] * head_lanes(odd) + value_more
        ones = jnp.ones((1, length), F32)
        lse = lse_ref[0, odd : odd + 1, :]
        queries = join_rows(
            qt_ref[half, :], extra_rows([ones] + [-part for part in split_three(lse)]), odd
        )
        delta = jnp.sum(
            ot_ref[half, :].astype(F32) * gt_ref[half, :].astype(F32), axis=0, keepdims=True
        )
        grads = join_rows(
            gt_ref[half, :], extra_rows([-part for part in split_three(delta)]), odd
        )
        for start in range(0, length, QBLOCK):
            columns = slice(start, start + QBLOCK)
            scores = add_bias(dot(keys, queries[:, columns]), table.at[odd], start, length)
            weights = jnp.exp2(scores)
            weights_all[:, columns] = weights.astype(BF16)
            grad_scores = weights * dot(values, grads[:, columns])
            grads_all[:, columns] = grad_scores.astype(BF16)
        grad_query_parts.append(dot(kt_ref[half, :], grads_all[...]) * 0.125)
        grad_values = dot_nt(weights_all[...], gt_ref[...])
        grad_keys = dot_nt(grads_all[...], qt_ref[...]) * LN2
        if odd:
            dv_ref[...] = jnp.where(first_lanes, even_values, grad_values).astype(BF16)
            dk_ref[...] = jnp.where(first_lanes, even_keys, grad_keys).astype(BF16)
        else:
            even_values, even_keys = grad_values, grad_keys
    dq_ref[...] = jnp.concatenate(grad_query_parts, axis=0).T.astype(BF16)


def attend_back(length_valid, offsets, qt, k, kt, v, ot, gt, lse):
    length = k.shape[0]
    turned = pl.BlockSpec((LANES, length), lambda p: (p, 0))
    natural = pl.BlockSpec((length, LANES), lambda p: (0, p))
    pair_rows = pl.BlockSpec((1, 2, 2 * length), lambda p: (p, 0, 0))
    natural_shape = jax.ShapeDtypeStruct((length, D), BF16)
    return pl.pallas_call(
        attend_back_kernel,
        grid=(HEADS // 2,),
        in_specs=[
            pl.BlockSpec(memory_space=pltpu.SMEM),
            pair_rows,
            turned,
            natural,
            turned,
            natural,
            turned,
            turned,
            pl.BlockSpec((1, 2, length), lambda p: (p, 0, 0)),
        ],
        out_specs=[natural] * 3,
        out_shape=[natural_shape] * 3,
        scratch_shapes=[
            pltpu.VMEM((2, LANES, 2 * length), F32),
            pltpu.VMEM((2, length, LANES), BF16),
            pltpu.VMEM((length, length), BF16),
            pltpu.VMEM((length, length), BF16),
        ],
        compiler_params=params(),
        name="attend_back",
    )(length_valid, offsets, qt, k, kt, v, ot, gt, lse)


def middle_kernel(
    length_ref,
    ot_ref,
    x_ref,
    cot_ref,
    gain_ref,
    w_out_ref,
    w_in_ref,
    w_down_ref,
    ar_out_ref,
    b_out_ref,
    ar_in_ref,
    b_in_ref,
    ar_down_ref,
    b_down_ref,
    out_ref,
    dmid_ref,
    gt_ref,
    sums_ref,
    dar_out_ref,
    db_out_ref,
    dar_in_ref,
    db_in_ref,
    dar_down_ref,
    db_down_ref,
    active,
    slope,
    sloped,
    grad_hidden,
    feeds,
):
    step = pl.program_id(0)

    @pl.when(step == 0)
    def _():
        for ref in (
            sums_ref,
            dar_out_ref,
            db_out_ref,
            dar_in_ref,
            db_in_ref,
            dar_down_ref,
            db_down_ref,
        ):
            ref[...] = jnp.zeros_like(ref)

    attended = ot_ref[...].T
    inputs = x_ref[...].astype(F32)
    gain = gain_ref[...]
    cot = cot_ref[...]

    packed_out = dot(attended, ar_out_ref[...])
    branch = dot(attended, w_out_ref[...])
    low_out, gates_out, mixed_out, natural = single_gates(packed_out)
    grad_mixed_down = dot_nt(cot, b_down_ref[...])
    branch = branch + dot(natural, b_out_ref[...])
    middle = inputs + branch
    inverse = rms_inverse(middle)
    normed = (middle * inverse * gain).astype(BF16)

    packed_in = dot(normed, ar_in_ref[...])
    low_in, gates_in, mixed_in, natural = single_gates(packed_in)

    def columns_of(index):
        return pl.ds(pl.multiple_of(index * CHUNK, CHUNK), CHUNK)

    def hidden_of(chunk):
        return dot(normed, w_in_ref[:, chunk]) + dot(natural, b_in_ref[:, chunk])

    def activate(chunk, values):
        grad_dense = dot_nt(cot, w_down_ref[chunk])
        square = values * values
        tangent = jnp.tanh(values * (GELU_SCALE + (GELU_SCALE * GELU_CUBIC) * square))
        half = 0.5 + 0.5 * tangent
        smooth = values * half
        active[:, chunk] = smooth.astype(BF16)
        steep = half + smooth * (1.0 - tangent) * (
            GELU_SCALE + (3.0 * GELU_SCALE * GELU_CUBIC) * square
        )
        slope[:, chunk] = steep.astype(BF16)
        sloped[:, chunk] = grad_dense * steep

    def forward_pair(pair, _):
        chunk_a = columns_of(2 * pair)
        chunk_b = columns_of(2 * pair + 1)
        hidden_a = hidden_of(chunk_a)
        hidden_b = hidden_of(chunk_b)
        activate(chunk_a, hidden_a)
        activate(chunk_b, hidden_b)
        return 0

    lax.fori_loop(0, FF // (2 * CHUNK), forward_pair, 0)

    packed_down = dot(active[...], ar_down_ref[...])
    def feed_part(index, _):
        part = pl.ds(pl.multiple_of(index * 256, 256), 256)
        feeds[:, part] = dot(active[...], w_down_ref[:, part])
        return 0

    lax.fori_loop(0, 3, feed_part, 0)
    feed = feeds[...]
    low_down, gates_down, mixed_down, natural = single_gates(packed_down)
    delta_down, natural_delta = single_deltas(grad_mixed_down, low_down, gates_down)
    db_down_ref[...] += dot(mixed_down[:UP_ROWS], cot)
    feed = feed + dot(natural, b_down_ref[...])
    output = middle + feed
    out_ref[...] = output.astype(BF16)

    def backward_chunk(index, _):
        chunk = columns_of(index)
        grad_low = dot_nt(natural_delta, ar_down_ref[chunk])
        grad_hidden[:, chunk] = (
            sloped[:, chunk] + grad_low * slope[:, chunk].astype(F32)
        ).astype(BF16)
        return 0

    lax.fori_loop(0, FF // CHUNK, backward_chunk, 0)
    dar_down_ref[...] += dot(delta_down[:DOWN_ROWS], active[...])

    rows = row_iota((MIDDLE_ROWS, 1)) + step * MIDDLE_ROWS
    valid = (rows < length_ref[0]).astype(F32)
    lane = lane_iota((8, LANES))
    totals = jnp.zeros((8, LANES), F32)
    for place, member in enumerate((inputs, branch, feed, output)):
        kept = member * valid
        totals = jnp.where(lane == place, jnp.sum(kept * kept), totals)
    sums_ref[...] += totals

    grad_mixed = dot_nt(grad_hidden[...], b_in_ref[...])
    def back_part(index, _):
        part = pl.ds(pl.multiple_of(index * 256, 256), 256)
        feeds[:, part] = dot_nt(grad_hidden[...], w_in_ref[part])
        return 0

    lax.fori_loop(0, 3, back_part, 0)
    grad_normed = feeds[...]
    delta_in, natural_delta = single_deltas(grad_mixed, low_in, gates_in)
    db_in_ref[...] += dot(mixed_in[:UP_ROWS], grad_hidden[...])
    grad_normed = grad_normed + dot_nt(natural_delta, ar_in_ref[...])
    dar_in_ref[...] += dot(delta_in[:DOWN_ROWS], normed)

    grad_middle = cot.astype(F32) + rms_backward(middle, gain, inverse, grad_normed)
    dmid_ref[...] = grad_middle
    grad_branch = grad_middle.astype(BF16)
    grad_mixed = dot_nt(grad_branch, b_out_ref[...])
    grad_attended = dot_nt(grad_branch, w_out_ref[...])
    delta_out, natural_delta = single_deltas(grad_mixed, low_out, gates_out)
    grad_attended = grad_attended + dot_nt(natural_delta, ar_out_ref[...])
    gt_ref[...] = grad_attended.astype(BF16).T
    dar_out_ref[...] += dot(delta_out[:DOWN_ROWS], attended)
    db_out_ref[...] += dot(mixed_out[:UP_ROWS], grad_branch)


def middle_part(length_valid, ot, x, cot, gain, w_out, w_in, w_down, adapters):
    length = x.shape[0]
    tile = pl.BlockSpec((MIDDLE_ROWS, D), lambda i: (i, 0))
    turned = pl.BlockSpec((D, MIDDLE_ROWS), lambda i: (0, i))
    grad_shapes = [
        jax.ShapeDtypeStruct(shape, F32)
        for fan_in, fan_out in FANS[3:]
        for shape in ((DOWN_ROWS, fan_in), (UP_ROWS, fan_out))
    ]
    out_shape = [
        jax.ShapeDtypeStruct((length, D), BF16),
        jax.ShapeDtypeStruct((length, D), F32),
        jax.ShapeDtypeStruct((D, length), BF16),
        jax.ShapeDtypeStruct((8, LANES), F32),
    ] + grad_shapes
    return pl.pallas_call(
        middle_kernel,
        grid=(length // MIDDLE_ROWS,),
        in_specs=[pl.BlockSpec(memory_space=pltpu.SMEM), turned, tile, tile]
        + [whole(member.shape) for member in (gain, w_out, w_in, w_down, *adapters)],
        out_specs=[tile, tile, turned] + [whole(member.shape) for member in out_shape[3:]],
        out_shape=out_shape,
        scratch_shapes=[
            pltpu.VMEM((MIDDLE_ROWS, FF), BF16),
            pltpu.VMEM((MIDDLE_ROWS, FF), BF16),
            pltpu.VMEM((MIDDLE_ROWS, FF), F32),
            pltpu.VMEM((MIDDLE_ROWS, FF), BF16),
            pltpu.VMEM((MIDDLE_ROWS, D), F32),
        ],
        compiler_params=params(),
        name="middle_part",
    )(length_valid, ot, x, cot, gain, w_out, w_in, w_down, *adapters)


def project_back_kernel(
    x_ref,
    gain_ref,
    w_ref,
    ar_ref,
    b_ref,
    zg_ref,
    dq_ref,
    dk_ref,
    dv_ref,
    dmid_ref,
    out_ref,
    dar_ref,
    db_ref,
):
    @pl.when(pl.program_id(0) == 0)
    def _():
        dar_ref[...] = jnp.zeros_like(dar_ref)
        db_ref[...] = jnp.zeros_like(db_ref)

    values = x_ref[...].astype(F32)
    gain = gain_ref[...]
    inverse = rms_inverse(values)
    normed = (values * inverse * gain).astype(BF16)
    lowrank = zg_ref[: 3 * COLS]
    gates = zg_ref[3 * COLS :]
    mixed = pad_rows(lowrank * gates, LANES).astype(BF16)
    grads = (dq_ref[...], dk_ref[...], dv_ref[...])
    columns = [slice(index * D, (index + 1) * D) for index in range(3)]
    grad_mixed = jnp.zeros((ROWS, LANES), F32)
    for grad, lanes in zip(grads, columns):
        grad_mixed = grad_mixed + dot_nt(grad, b_ref[:, lanes])
    grad_normed = jnp.zeros((ROWS, D), F32)
    for grad, lanes in zip(grads, columns):
        grad_normed = grad_normed + dot_nt(grad, w_ref[:, lanes])
        db_ref[:, lanes] += dot(mixed, grad)
    turned = grad_mixed.T
    parts = []
    for first in range(0, 3 * COLS, COLS):
        rows = slice(first, first + COLS)
        parts.append(gate_grads(turned[rows], lowrank[rows], gates[rows]))
    delta = jnp.concatenate([part[0] for part in parts] + [part[1] for part in parts], axis=0)
    delta = pad_rows(delta, 2 * LANES).astype(BF16)
    grad_normed = grad_normed + dot_nt(delta.T, ar_ref[...])
    dar_ref[...] += dot(delta, normed)
    out_ref[...] = dmid_ref[...] + rms_backward(values, gain, inverse, grad_normed)


def project_back(x, gain, w_qkv, ar_qkv, b_qkv, zg, dq, dk, dv, dmid):
    length = x.shape[0]
    tile = pl.BlockSpec((ROWS, D), lambda i: (i, 0))
    out_shape = [
        jax.ShapeDtypeStruct((length, D), F32),
        jax.ShapeDtypeStruct((2 * LANES, D), F32),
        jax.ShapeDtypeStruct((LANES, 3 * D), F32),
    ]
    return pl.pallas_call(
        project_back_kernel,
        grid=(length // ROWS,),
        in_specs=[
            tile,
            whole((1, D)),
            whole(w_qkv.shape),
            whole(ar_qkv.shape),
            whole(b_qkv.shape),
            pl.BlockSpec((6 * COLS, ROWS), lambda i: (0, i)),
            tile,
            tile,
            tile,
            tile,
        ],
        out_specs=[tile] + [whole(member.shape) for member in out_shape[1:]],
        out_shape=out_shape,
        compiler_params=params(),
        name="project_back",
    )(x, gain, w_qkv, ar_qkv, b_qkv, zg, dq, dk, dv, dmid)


PARAM_ROWS = sum((COLS + EXPERTS) * fan_in + COLS * fan_out for fan_in, fan_out in FANS) // LANES


def piece_rows():
    result = []
    row = 0
    for fan_in, fan_out in FANS:
        starts = []
        for count in (fan_in * COLS, COLS * fan_out, fan_in * EXPERTS):
            starts.append(row)
            row += count // LANES
        result.append(tuple(starts))
    return result


def shard_rows(count):
    return -(-count // (LANES * 16)) * 16


def align_in(flat_ref, shard, start):
    first, shift = divmod(start, LANES)
    rows = shard.shape[0]
    if shift == 0:
        flat_ref[first : first + rows] = shard
        return
    turned = pltpu.roll(shard, shift, 1)
    lane = lane_iota((1, LANES))
    zeros = jnp.zeros((8, LANES), F32)
    upper = jnp.concatenate([turned, zeros], axis=0)
    lower = pltpu.roll(upper, 1, 0)
    kept = flat_ref[first : first + 8]
    merged = jnp.where(lane >= shift, upper, lower)
    inside = (row_iota((8, LANES)) == 0) & (lane_iota((8, LANES)) < shift)
    flat_ref[first : first + 8] = jnp.where(inside, kept, merged[:8])
    flat_ref[first + 8 : first + 8 + rows] = merged[8:]


def align_out(flat_ref, rows, start):
    first, shift = divmod(start, LANES)
    if shift == 0:
        return flat_ref[first : first + rows]
    block = flat_ref[first : first + rows + 8]
    turned = pltpu.roll(block, LANES - shift, 1)
    below = pltpu.roll(turned, rows + 7, 0)
    lane = lane_iota((1, LANES))
    return jnp.where(lane < LANES - shift, turned, below)[:rows]


def narrow_to_rows(flat_ref, base, fan_in, width, place, out_ref):
    period = 640 // width
    groups = fan_in // period
    lines = [flat_ref[pl.ds(base + k, groups, stride=5), :] for k in range(5)]
    lane = lane_iota((1, LANES))
    for b in range(period):
        first, shift = divmod(width * b, LANES)
        amount = (place - shift) % LANES
        value = lines[first] if amount == 0 else pltpu.roll(lines[first], amount, 1)
        if shift + width > LANES:
            value = jnp.where(
                lane < place + LANES - shift, value, pltpu.roll(lines[first + 1], amount, 1)
            )
        inside = (lane >= place) & (lane < place + width)
        out_ref[pl.ds(b, groups, stride=period), :] = jnp.where(inside, value, 0.0)


def rows_to_narrow(in_ref, fan_in, width, place, flat_ref, base):
    period = 640 // width
    groups = fan_in // period
    lane = lane_iota((1, LANES))
    lines = [jnp.zeros((groups, LANES), F32) for _ in range(5)]
    for b in range(period):
        first, shift = divmod(width * b, LANES)
        amount = (shift - place) % LANES
        value = in_ref[pl.ds(b, groups, stride=period), :]
        value = value if amount == 0 else pltpu.roll(value, amount, 1)
        inside = (lane >= shift) & (lane < shift + width)
        lines[first] = jnp.where(inside, value, lines[first])
        if shift + width > LANES:
            lines[first + 1] = jnp.where(lane < shift + width - LANES, value, lines[first + 1])
    for k in range(5):
        flat_ref[pl.ds(base + k, groups, stride=5), :] = lines[k]


def spread_matrix(place):
    row = row_iota((LANES, LANES))
    lane = lane_iota((LANES, LANES)) - place
    hit = (lane >= RANK * row) & (lane < RANK * row + RANK) & (row < EXPERTS)
    return jnp.where(hit, 1.0, 0.0).astype(BF16)


def unpack_kernel(
    count,
    shards_ref,
    ar_qkv_ref,
    b_qkv_ref,
    ar_out_ref,
    b_out_ref,
    ar_in_ref,
    b_in_ref,
    ar_down_ref,
    b_down_ref,
    flat,
    down,
    router,
):
    shards = shards_ref.shape[0]
    for index in range(shards):
        align_in(flat, shards_ref[index].astype(F32), index * count)
    starts = piece_rows()

    def ups(base, fan_out, first, out_ref, column):
        width = fan_out // LANES
        above = jnp.zeros((first, LANES), F32)
        below = jnp.zeros((LANES - COLS - first, LANES), F32)
        for k in range(width):
            part = flat[pl.ds(base + k, COLS, stride=width), :]
            parts = [part, below] if first == 0 else [above, part, below]
            lanes = slice(column + k * LANES, column + (k + 1) * LANES)
            out_ref[:, lanes] = jnp.concatenate(parts, axis=0).astype(BF16)

    packed = [jnp.zeros((D, LANES), F32) for _ in range(2)]
    for index in range(3):
        base_a, base_b, base_r = starts[index]
        narrow_to_rows(flat, base_a, D, COLS, index * COLS, down)
        narrow_to_rows(flat, base_r, D, EXPERTS, 0, router)
        packed[0] = packed[0] + down[:D]
        for half in range(2):
            matrix = spread_matrix((3 + index) * COLS - half * LANES)
            packed[half] = packed[half] + dot(router[:D].astype(BF16), matrix)
        ups(base_b, D, index * COLS, b_qkv_ref, index * D)
    ar_qkv_ref[:, :LANES] = packed[0].astype(BF16)
    ar_qkv_ref[:, LANES:] = packed[1].astype(BF16)
    members = ((ar_out_ref, b_out_ref), (ar_in_ref, b_in_ref), (ar_down_ref, b_down_ref))
    for index, (ar_ref, b_ref) in zip(range(3, 6), members):
        base_a, base_b, base_r = starts[index]
        fan_in, fan_out = FANS[index]
        narrow_to_rows(flat, base_a, fan_in, COLS, 0, down)
        narrow_to_rows(flat, base_r, fan_in, EXPERTS, 0, router)
        wide = dot(router[:fan_in].astype(BF16), spread_matrix(COLS))
        ar_ref[...] = (down[:fan_in] + wide).astype(BF16)
        ups(base_b, fan_out, 0, b_ref, 0)


def unpack(shards, count):
    rows = shards.shape[1]
    shapes = ((D, 2 * LANES), (LANES, 3 * D), (D, LANES), (LANES, D), (D, LANES), (LANES, FF), (FF, LANES), (LANES, D))
    return pl.pallas_call(
        functools.partial(unpack_kernel, count),
        in_specs=[pl.BlockSpec(memory_space=pltpu.VMEM)],
        out_specs=[pl.BlockSpec(memory_space=pltpu.VMEM)] * len(shapes),
        out_shape=[jax.ShapeDtypeStruct(shape, BF16) for shape in shapes],
        scratch_shapes=[
            pltpu.VMEM((PARAM_ROWS + rows + 20, LANES), F32),
            pltpu.VMEM((FF, LANES), F32),
            pltpu.VMEM((FF, LANES), F32),
        ],
        compiler_params=params(),
        name="unpack",
    )(shards)


def gather_matrix(place):
    row = row_iota((LANES, LANES)) - place
    lane = lane_iota((LANES, LANES))
    return jnp.where((row == RANK * lane) & (lane < EXPERTS), 1.0, 0.0).astype(BF16)


def assemble_kernel(
    count,
    dar_qkv_ref,
    db_qkv_ref,
    dar_out_ref,
    db_out_ref,
    dar_in_ref,
    db_in_ref,
    dar_down_ref,
    db_down_ref,
    shards_ref,
    flat,
    down,
    router,
):
    starts = piece_rows()

    def ups(base, fan_out, first, grad_ref, column):
        width = fan_out // LANES
        for k in range(width):
            lanes = slice(column + k * LANES, column + (k + 1) * LANES)
            flat[pl.ds(base + k, COLS, stride=width), :] = grad_ref[first : first + COLS, lanes]

    def routers(packed, place):
        matrix = gather_matrix(place)
        high = packed.astype(BF16)
        return dot(high, matrix) + dot((packed - high.astype(F32)).astype(BF16), matrix)

    members = (
        (3, dar_out_ref, db_out_ref),
        (4, dar_in_ref, db_in_ref),
        (5, dar_down_ref, db_down_ref),
    )
    for index, dar_ref, db_ref in members:
        base_a, base_b, base_r = starts[index]
        fan_in, fan_out = FANS[index]
        packed = pad_rows(dar_ref[...], LANES).T
        down[:fan_in] = packed
        rows_to_narrow(down, fan_in, COLS, 0, flat, base_a)
        router[:fan_in] = routers(packed, COLS)
        rows_to_narrow(router, fan_in, EXPERTS, 0, flat, base_r)
        ups(base_b, fan_out, 0, db_ref, 0)
    down[:D] = dar_qkv_ref[:LANES].T
    first_router = 3 * COLS
    packed_router = dar_qkv_ref[first_router : first_router + LANES].T
    for index in range(3):
        base_a, base_b, base_r = starts[index]
        rows_to_narrow(down, D, COLS, index * COLS, flat, base_a)
        router[:D] = routers(packed_router, index * COLS)
        rows_to_narrow(router, D, EXPERTS, 0, flat, base_r)
        ups(base_b, D, index * COLS, db_qkv_ref, index * D)
    shards, rows = shards_ref.shape[0], shards_ref.shape[1]
    for index in range(shards):
        shards_ref[index] = align_out(flat, rows, index * count)


def assemble(grads, shards, count):
    rows = shard_rows(count)
    return pl.pallas_call(
        functools.partial(assemble_kernel, count),
        in_specs=[pl.BlockSpec(memory_space=pltpu.VMEM)] * len(grads),
        out_specs=pl.BlockSpec(memory_space=pltpu.VMEM),
        out_shape=jax.ShapeDtypeStruct((shards, rows, LANES), F32),
        scratch_shapes=[
            pltpu.VMEM((PARAM_ROWS + rows + 20, LANES), F32),
            pltpu.VMEM((FF, LANES), F32),
            pltpu.VMEM((FF, LANES), F32),
        ],
        compiler_params=params(),
        name="assemble",
    )(*grads)


MESH = pl.DeviceIdType.MESH


def place_of(axes, sizes):
    me = lax.axis_index(axes[0]) * sizes[1] + lax.axis_index(axes[1])

    def coordinates(number):
        return (number // sizes[1], number % sizes[1])

    return me, coordinates


def partners_of(me):
    low = me % 8
    core = low % 2
    y = (low // 2) % 2
    x = low // 4
    over_x = low + 4 * (1 - 2 * x)
    over_y = low + 2 * (1 - 2 * y)
    first = over_x * (1 - core) + over_y * core
    second = over_y * (1 - core) + over_x * core
    both = first + second - low
    other = 1 - 2 * core
    return low, first, second, both, other, over_x, over_y


def greet(peers):
    barrier = pltpu.get_barrier_semaphore()
    for peer in peers:
        pl.semaphore_signal(barrier, inc=1, device_id=peer, device_id_type=MESH)
    pl.semaphore_wait(barrier, len(peers))


def gather_kernel(axes, sizes, shard_ref, out_ref, send, receive, local):
    me, coordinates = place_of(axes, sizes)
    groups = out_ref.shape[0]
    group = me // 8
    low, first, second, both, other, over_x, over_y = partners_of(me)

    def device(group_index, low_index):
        return coordinates(group_index * 8 + low_index)

    others = [(group + step) % groups for step in range(1, groups)]
    peers = [device(index, low) for index in others]
    peers += [device(group, partner) for partner in (first, second, low + other)]
    greet(peers)
    counter = [0]

    def start(source, target, peer):
        index = counter[0]
        counter[0] += 1
        copy = pltpu.make_async_remote_copy(
            src_ref=source,
            dst_ref=target,
            send_sem=send.at[index],
            recv_sem=receive.at[index],
            device_id=peer,
            device_id_type=MESH,
        )
        copy.start()
        return copy

    own = pltpu.make_async_copy(shard_ref, out_ref.at[group, low], local)
    own.start()
    around = [start(shard_ref, out_ref.at[group, low], device(index, low)) for index in others]
    own.wait()
    for copy in around:
        copy.wait()

    def push(part, partner):
        return start(out_ref.at[:, part], out_ref.at[:, part], device(group, partner))

    one = push(low, first)
    two = push(low, second)
    core_own = push(low, low + other)
    one.wait()
    three = push(first, second)
    core_first = push(first, low + other)
    two.wait()
    core_second = push(second, low + other)
    three.wait()
    core_both = push(both, low + other)
    for copy in (core_own, core_first, core_second, core_both):
        copy.wait()


def gather(shard, axes, sizes):
    groups = sizes[0] * sizes[1] // 8
    copies = groups - 1 + 7
    return pl.pallas_call(
        functools.partial(gather_kernel, axes, sizes),
        in_specs=[pl.BlockSpec(memory_space=pltpu.VMEM)],
        out_specs=pl.BlockSpec(memory_space=pltpu.VMEM),
        out_shape=jax.ShapeDtypeStruct((groups, 8, *shard.shape), shard.dtype),
        scratch_shapes=[
            pltpu.SemaphoreType.DMA((copies,)),
            pltpu.SemaphoreType.DMA((copies,)),
            pltpu.SemaphoreType.DMA,
        ],
        compiler_params=params(collective_id=0, has_side_effects=True),
        name="gather",
    )(shard)


def reduce_kernel(
    axes, sizes, parts_ref, sums_ref, out_ref, total_ref, outbox, inbox, near_out, near_in, far_in, own, send, receive
):
    me, coordinates = place_of(axes, sizes)
    groups = parts_ref.shape[0]
    group = me // 8
    low, first, second, both, other, over_x, over_y = partners_of(me)

    def device(group_index, low_index):
        return coordinates(group_index * 8 + low_index)

    others = [(group + step) % groups for step in range(1, groups)]
    peers = [device(index, low) for index in others]
    peers += [device(group, partner) for partner in (first, second, low + other)]
    greet(peers)
    counter = [0]

    def start(source, target, peer):
        index = counter[0]
        counter[0] += 1
        copy = pltpu.make_async_remote_copy(
            src_ref=source,
            dst_ref=target,
            send_sem=send.at[index],
            recv_sem=receive.at[index],
            device_id=peer,
            device_id_type=MESH,
        )
        copy.start()
        return copy

    def push(slot, value, partner):
        outbox[slot] = value.astype(BF16)
        return start(outbox.at[slot], inbox.at[slot], device(group, partner))

    def push_sums(slot, value, partner):
        near_out[slot] = value
        return start(near_out.at[slot], near_in.at[slot], device(group, partner))

    mate = low + other
    sums = sums_ref[...]
    sums_core = push_sums(0, sums, mate)
    core = [
        push(slot, parts_ref[:, part + other], mate)
        for slot, part in enumerate((first, both, second, low))
    ]
    core[0].wait()
    half_second = parts_ref[:, second] + inbox[0].astype(F32)
    to_second = push(4, half_second, second)
    core[1].wait()
    half_both = parts_ref[:, both] + inbox[1].astype(F32)
    to_both = push(5, half_both, second)
    sums_core.wait()
    sums = sums + near_in[0]
    sums_x = push_sums(1, sums, over_x)
    core[2].wait()
    half_first = parts_ref[:, first] + inbox[2].astype(F32)
    core[3].wait()
    half_low = parts_ref[:, low] + inbox[3].astype(F32)
    to_both.wait()
    quarter_first = half_first + inbox[5].astype(F32)
    to_first = push(6, quarter_first, first)
    sums_x.wait()
    sums = sums + near_in[1]
    sums_y = push_sums(2, sums, over_y)
    to_second.wait()
    half_low = half_low + inbox[4].astype(F32)
    to_first.wait()
    own[...] = half_low + inbox[6].astype(F32)
    outbox[7] = own[...].astype(BF16)
    around = [
        start(outbox.at[7, index], far_in.at[step], device(index, low))
        for step, index in enumerate(others)
    ]
    sums_y.wait()
    near_out[3] = sums + near_in[2]
    around_sums = [
        start(near_out.at[3], near_in.at[4 + group], device(index, low))
        for index in others
    ]
    near_in[4 + group] = near_out[3]
    total = own[group]
    for step, copy in enumerate(around):
        copy.wait()
        total = total + far_in[step].astype(F32)
    out_ref[...] = total
    for copy in around_sums:
        copy.wait()
    whole_sum = near_in[4]
    for index in range(1, groups):
        whole_sum = whole_sum + near_in[4 + index]
    total_ref[...] = whole_sum


def reduce_scatter(parts, sums, axes, sizes):
    groups, _, rows, lanes = parts.shape
    copies = 7 + 3 + 2 * (groups - 1)
    return pl.pallas_call(
        functools.partial(reduce_kernel, axes, sizes),
        in_specs=[pl.BlockSpec(memory_space=pltpu.VMEM)] * 2,
        out_specs=[pl.BlockSpec(memory_space=pltpu.VMEM)] * 2,
        out_shape=[
            jax.ShapeDtypeStruct((rows, lanes), F32),
            jax.ShapeDtypeStruct(sums.shape, F32),
        ],
        scratch_shapes=[
            pltpu.VMEM((8, groups, rows, lanes), BF16),
            pltpu.VMEM((7, groups, rows, lanes), BF16),
            pltpu.VMEM((4, *sums.shape), F32),
            pltpu.VMEM((4 + groups, *sums.shape), F32),
            pltpu.VMEM((groups - 1, rows, lanes), BF16),
            pltpu.VMEM((groups, rows, lanes), F32),
            pltpu.SemaphoreType.DMA((copies,)),
            pltpu.SemaphoreType.DMA((copies,)),
        ],
        compiler_params=params(collective_id=1, has_side_effects=True),
        name="reduce_scatter",
    )(parts, sums)


def per_device(
    tokens,
    lengths,
    buckets,
    rel_table,
    gain_attn,
    gain_ff,
    w_qkv,
    w_out,
    w_in,
    w_down,
    adapters,
    cotangent,
    axes,
    sizes,
):
    seq_count, length, width = tokens.shape
    x = tokens.reshape(length, width)
    cot = cotangent.reshape(length, width)
    devices = sizes[0] * sizes[1]
    count = adapters.shape[0]
    rows = shard_rows(count)
    shard = jnp.pad(adapters, (0, rows * LANES - count)).reshape(rows, LANES)
    if devices == 1:
        shards = shard[None]
    else:
        shards = gather(shard, axes, sizes).reshape(devices, rows, LANES)
    ar_qkv, b_qkv, *rest = unpack(shards, count)
    gain_first = gain_attn.reshape(1, width)
    gain_second = gain_ff.reshape(1, width)

    reversed_buckets = jnp.pad(buckets[::-1], (0, 1))
    hits = (jnp.arange(rel_table.shape[0])[:, None] == reversed_buckets[None, :]).astype(F32)
    offsets = jnp.dot(rel_table.T * LOG2E, hits, precision=lax.Precision.HIGHEST)
    offsets = offsets.reshape(HEADS // 2, 2, 2 * length)

    qt, k, kt, v, vt, zg = project(x, gain_first, w_qkv, ar_qkv, b_qkv)
    ot, lse = attend(lengths, offsets, qt, k, vt)
    block_out, dmid, gt, sums, *grads = middle_part(
        lengths, ot, x, cot, gain_second, w_out, w_in, w_down, rest
    )
    dq, dk, dv = attend_back(lengths, offsets, qt, k, kt, v, ot, gt, lse)
    tokens_grad, dar_qkv, db_qkv = project_back(
        x, gain_first, w_qkv, ar_qkv, b_qkv, zg, dq, dk, dv, dmid
    )

    parts = assemble((dar_qkv, db_qkv, *grads), devices, count)
    sums = jnp.where(jnp.arange(LANES)[None, :] == 4, jnp.sum(lengths).astype(F32), sums)
    if devices == 1:
        mine, sums = parts[0], sums
    else:
        parts = parts.reshape(devices // 8, 8, rows, LANES)
        mine, sums = reduce_scatter(parts, sums, axes, sizes)
    grad_shard = mine.reshape(-1)[:count]
    root_squares = jnp.sqrt(sums[0, :4] / (sums[0, 4] * width))
    return (
        block_out.reshape(tokens.shape),
        tokens_grad.reshape(tokens.shape),
        grad_shard,
        root_squares,
    )


def solution(mesh):
    axes = tuple(mesh.axis_names)
    sizes = tuple(mesh.shape[axis] for axis in axes)
    sequence = P(axes, None, None)
    placed = (
        sequence,
        P(axes),
        P(),
        P(),
        P(),
        P(),
        P(),
        P(),
        P(),
        P(),
        P(axes),
        sequence,
    )
    return jax.shard_map(
        functools.partial(per_device, axes=axes, sizes=sizes),
        mesh=mesh,
        in_specs=placed,
        out_specs=(sequence, sequence, P(axes), P()),
        check_vma=False,
    )
```

profile of v0, /device:TPU:0, one launch (start us, length us, event | category | flops | bytes accessed | tf_op | source)
XLA Modules:
  0.0 207.2 jit_solution(10255891131769406509)
XLA Ops:
  1.3 0.8 reverse
  2.0 0.1 slice.14
  2.1 0.9 fusion
  3.0 0.7 reshape.54.off_ref
  3.7 1.3 reshape.56.gain_ref
  5.0 1.4 pad_bitcast_fusion.shard_ref
  6.4 23.2 %gather.1 = bf16[4,8,160,128]{3,2,1,0:T(8,128)(2,1)} custom-call(bf16[160,128]{1,0:T(8,128)(2,1)} %pad_bitcast_fusion.shard_ref), custom_call_target="tpu_custom_call" | custom-call | tf_op jit(solution)/shard_map/gather/pallas_call | solution.py:972
  29.6 8.7 %unpack.1 = (bf16[768,256]{1,0:T(8,128)(2,1)}, bf16[128,2304]{1,0:T(8,128)(2,1)}, bf16[768,128]{1,0:T(8,128)(2,1)}, bf16[128,768]{1,0:T(8,128)(2,1)}, bf16[768,1...) custom-call(bf16[32,160,128]{2,1,0:T(8,128)(2,1)} %bitcast.18), custom_call_target="tpu_custom_call" | custom-call | tf_op jit(solution)/shard_map/unpack/pallas_call | solution.py:789
  38.3 11.8 %project.1 = (bf16[768,1024]{1,0:T(8,128)(2,1)}, bf16[1024,768]{1,0:T(8,128)(2,1)}, bf16[768,1024]{1,0:T(8,128)(2,1)}, bf16[1024,768]{1,0:T(8,128)(2,1)}, bf16[7...) custom-call(bf16[1024,768]{1,0:T(8,128)(2,1)} %bitcast.14, f32[1,768]{1,0:T(1,128)} %reshape.56.gain_ref, ...), custom_call_target="tpu_custom_call" | custom-call | tf_op jit(solution)/shard_map/project/pallas_call | solution.py:144
  50.1 0.0 copy-start
  50.1 19.7 %attend.1 = (bf16[768,1024]{1,0:T(8,128)(2,1)}, f32[6,2,1024]{2,1,0:T(2,128)}) custom-call(s32[1]{0:T(128)S(6)} %copy.16.length_ref, f32[6,2,2048]{2,1,0:T(2,128)} %reshape.54.off_ref, bf16[768,1024]{1,0:T(8,128)(2,1)} %get-tuple-element.40.qt_ref, bf16[1024,768]{1,0:T(8,128)(2,1)} %get-tuple-element.41.k_ref, bf16[768,1024]{1,0:T(8,128)(2,1)} %get-tuple-element.42.vt_ref), custom_call_target="tpu_custom_call" | custom-call | tf_op jit(solution)/shard_map/attend/pallas_call | solution.py:257
  69.8 0.0 copy-done
  69.8 0.6 reshape.60.gain_ref
  70.4 54.3 %middle_part.1 = (bf16[1024,768]{1,0:T(8,128)(2,1)}, f32[1024,768]{1,0:T(8,128)}, bf16[768,1024]{1,0:T(8,128)(2,1)}, f32[8,128]{1,0:T(8,128)}, f32[80,768]{1,0:T...) custom-call(s32[1]{0:T(128)S(6)} %copy.16.length_ref, ...), custom_call_target="tpu_custom_call" | custom-call | tf_op jit(solution)/shard_map/middle_part/pallas_call | solution.py:546
  124.7 34.6 %attend_back.1 = (bf16[1024,768]{1,0:T(8,128)(2,1)}, bf16[1024,768]{1,0:T(8,128)(2,1)}, bf16[1024,768]{1,0:T(8,128)(2,1)}) custom-call(s32[1]{0:T(128)S(6)} %copy.16.length_ref, f32[6,2,2048]{2,1,0:T(2,128)} %reshape.54.off_ref, bf16[768,1024]{1,0:T(8,128)(2,1)} %get-tuple-element.40.qt_ref, bf16[1024,768]{1,0:T(8,128)(2,1)} %get-tuple-element.41.k_ref, ...), custom_call_target="tpu_custom_call" | custom-call | tf_op jit(solution)/shard_map/attend_back/pallas_call | solution.py:351
  159.2 12.6 %project_back.1 = (f32[1024,768]{1,0:T(8,128)}, f32[256,768]{1,0:T(8,128)}, f32[128,2304]{1,0:T(8,128)}) custom-call(bf16[1024,768]{1,0:T(8,128)(2,1)} %bitcast.16, f32[1,768]{1,0:T(1,128)} %reshape.56.gain_ref, bf16[768,2304]{1,0:T(8,128)(2,1)} %w_ref.3, bf16[768,256]{1,0:T(8,128)(2,1)} %get-tuple-element.38.ar_ref, ...), custom_call_target="tpu_custom_call" | custom-call | tf_op jit(solution)/shard_map/project_back/pallas_call | solution.py:621
  171.9 0.0 copy-start.1
  171.9 9.6 %assemble.1 = f32[32,160,128]{2,1,0:T(8,128)} custom-call(f32[256,768]{1,0:T(8,128)} %get-tuple-element.61.dar_qkv_ref, f32[128,2304]{1,0:T(8,128)} %get-tuple-element.62.db_qkv_ref, f32[80,768]{1,0:T(8,128)} %get-tuple-element.63.dar_out_ref, f32[48,768]{1,0:T(8,128)} %get-tuple-element.64.db_out_ref, f32[80,768]{1,0:T(8,128)} %get-tuple-element.65.dar_in_ref, ...), custom_call_target="tpu_custom_call" | custom-call | tf_op jit(solution)/shard_map/assemble/pallas_call | solution.py:868
  181.4 0.0 copy-done.1
  181.4 0.6 broadcast_select_fusion.sums_ref
  182.0 20.5 %reduce_scatter.1 = (f32[160,128]{1,0:T(8,128)}, f32[8,128]{1,0:T(8,128)}) custom-call(f32[4,8,160,128]{3,2,1,0:T(8,128)} %bitcast.17, f32[8,128]{1,0:T(8,128)} %broadcast_select_fusion.sums_ref), custom_call_target="tpu_custom_call" | custom-call | tf_op jit(solution)/shard_map/reduce_scatter/pallas_call | solution.py:1084
  202.5 1.5 slice.12
  204.1 1.3 slice.11
  206.0 1.2 sqrt_bitcast_fusion
  (2 shorter events, 0.0 us)
Async XLA Ops:
  50.1 19.7 %copy-start = (f32[768]{0:T(1024)S(1)}, f32[768]{0:T(1024)}, u32[]{:S(2)}) copy-start(f32[768]{0:T(1024)} %param.17) | copy-start | bytes 9220
  171.9 9.6 %copy-start.1 = (f32[8,128]{1,0:T(8,128)S(1)}, f32[8,128]{1,0:T(8,128)}, u32[]{:S(2)}) copy-start(f32[8,128]{1,0:T(8,128)} %get-tuple-element.69) | copy-start | bytes 12292
where the time goes:
time: 208 us; the launch traced here: 207 us
  Pallas kernels  195 us (94%)
  local copies, waits for them, and re-layouts  7.58 us (4%)
    pallas_call x1, Pallas kernels, middle_part(): pl.pallas_call(middle_kernel, grid=(length // MIDDLE_ROWS,), in_specs=[pl...  54.3 us
    pallas_call x1, Pallas kernels, attend_back(): pl.pallas_call(attend_back_kernel, grid=(HEADS // 2,), in_specs=[pl.Block...  34.6 us
    pallas_call x1, Pallas kernels, gather(): pl.pallas_call(functools.partial(gather_kernel, axes, sizes), in_specs=[p...  23.2 us
    pallas_call x1, Pallas kernels, reduce_scatter(): pl.pallas_call(functools.partial(reduce_kernel, axes, sizes), in_specs=[p...  20.5 us
    pallas_call x1, Pallas kernels, attend(): pl.pallas_call(attend_kernel, grid=(HEADS // 2,), in_specs=[pl.BlockSpec(...  19.7 us
    pallas_call x1, Pallas kernels, project_back(): pl.pallas_call(project_back_kernel, grid=(length // ROWS,), in_specs=[til...  12.6 us
    pallas_call x1, Pallas kernels, project(): pl.pallas_call(project_kernel, grid=(length // ROWS,), in_specs=[tile, wh...  11.8 us
    pallas_call x1, Pallas kernels, assemble(): pl.pallas_call(functools.partial(assemble_kernel, count), in_specs=[pl.Bl...  9.57 us

commit v1 on v0

--- a/solution.py
+++ b/solution.py
@@ -111,8 +111,32 @@
 
 
 def project_kernel(
-    x_ref, gain_ref, w_ref, ar_ref, b_ref, qt_ref, k_ref, kt_ref, v_ref, vt_ref, zg_ref
+    link,
+    shard_ref,
+    x_ref,
+    gain_ref,
+    w_ref,
+    ar_ref,
+    b_ref,
+    qt_ref,
+    k_ref,
+    kt_ref,
+    v_ref,
+    vt_ref,
+    zg_ref,
+    shards_ref,
+    landing,
+    send,
+    receive,
+    local,
 ):
+    step = pl.program_id(0)
+    if link is not None:
+        axes, sizes, span = link
+        ring = Ring(axes, sizes, send, receive)
+        phases = gather_phases(ring, span, shard_ref, landing, local)
+        for turn, phase in enumerate(phases[:4]):
+            pl.when(step == turn)(phase)
     values = x_ref[...].astype(F32)
     normed = (values * rms_inverse(values) * gain_ref[...]).astype(BF16)
     packed = dot(normed, ar_ref[...]).T
@@ -134,17 +158,31 @@
             natural[...] = low
             turned[...] = low.T
 
-
-def project(x, gain, w_qkv, ar_qkv, b_qkv):
+    if link is not None:
+
+        @pl.when(step == pl.num_programs(0) - 1)
+        def _():
+            phases[4]()
+            shards_ref[...] = landing[...]
+
+
+def project(x, gain, w_qkv, ar_qkv, b_qkv, shard, axes, sizes, span):
     length = x.shape[0]
+    devices = sizes[0] * sizes[1]
+    link = None if devices == 1 else (axes, sizes, span)
+    groups = max(devices // 8, 1)
+    landing = (max(span[1] - span[0], 1), 8, *shard.shape)
+    if link is None:
+        landing = (1, 8, 16, LANES)
     tile = pl.BlockSpec((ROWS, D), lambda i: (i, 0))
     turned = pl.BlockSpec((D, ROWS), lambda i: (0, i))
     natural_shape = jax.ShapeDtypeStruct((length, D), BF16)
     turned_shape = jax.ShapeDtypeStruct((D, length), BF16)
     return pl.pallas_call(
-        project_kernel,
+        functools.partial(project_kernel, link),
         grid=(length // ROWS,),
         in_specs=[
+            whole(shard.shape),
             tile,
             whole((1, D)),
             whole(w_qkv.shape),
@@ -158,6 +196,7 @@
             tile,
             turned,
             pl.BlockSpec((6 * COLS, ROWS), lambda i: (0, i)),
+            whole(landing),
         ],
         out_shape=[
             turned_shape,
@@ -166,10 +205,14 @@
             natural_shape,
             turned_shape,
             jax.ShapeDtypeStruct((6 * COLS, length), F32),
-        ],
-        compiler_params=params(),
+            jax.ShapeDtypeStruct(landing, BF16),
+        ],
+        scratch_shapes=[pltpu.VMEM(landing, BF16), *gather_semaphores(groups)],
+        compiler_params=params()
+        if link is None
+        else params(collective_id=1, has_side_effects=True),
         name="project",
-    )(x, gain, w_qkv, ar_qkv, b_qkv)
+    )(shard, x, gain, w_qkv, ar_qkv, b_qkv)
 
 
 def bias_table(offset_row, length):
@@ -229,7 +272,8 @@
 
     for odd in range(2):
         half = slice(odd * HDIM, (odd + 1) * HDIM)
-        table[odd] = bias_table(off_ref[0, odd : odd + 1, :], length)
+        row = 2 * pl.program_id(0) + odd
+        table[odd] = bias_table(off_ref[pl.ds(row, 1), :], length)
         keys = k_ref[...] * head_lanes(odd) + key_more[odd]
         ones = jnp.ones((1, length), F32)
         queries = join_rows(qt_ref[half, :], extra_rows([ones]), odd)
@@ -253,13 +297,12 @@
     length = k.shape[0]
     turned = pl.BlockSpec((LANES, length), lambda p: (p, 0))
     natural = pl.BlockSpec((length, LANES), lambda p: (0, p))
-    pair_rows = pl.BlockSpec((1, 2, 2 * length), lambda p: (p, 0, 0))
     return pl.pallas_call(
         attend_kernel,
         grid=(HEADS // 2,),
         in_specs=[
             pl.BlockSpec(memory_space=pltpu.SMEM),
-            pair_rows,
+            whole(offsets.shape),
             turned,
             natural,
             turned,
@@ -279,6 +322,7 @@
 
 
 def attend_back_kernel(
+    link,
     length_ref,
     off_ref,
     qt_ref,
@@ -288,15 +332,41 @@
     ot_ref,
     gt_ref,
     lse_ref,
+    parts_ref,
+    sums_ref,
     dq_ref,
     dk_ref,
     dv_ref,
+    rest_ref,
+    roots_ref,
     table,
     key_more,
     weights_all,
     grads_all,
+    *scratch,
 ):
     length = k_ref.shape[0]
+    step = pl.program_id(0)
+
+    def finish_sums(total):
+        roots_ref[...] = jnp.sqrt(total / (total[:, 4:5] * D))
+
+    if link is None:
+        finish_sums(sums_ref[...])
+    else:
+        axes, sizes, span = link
+        *boxes, total, near_out, near_in, send, receive = scratch
+        ring = Ring(axes, sizes, send, receive)
+        phases = reduce_phases(
+            ring, span, parts_ref, (*boxes, total), sums_ref, (near_out, near_in)
+        )
+        for turn, phase in enumerate(phases[:4]):
+            pl.when(step == turn)(phase)
+
+        @pl.when(step == pl.num_programs(0) - 1)
+        def _():
+            phases[4](finish_sums)
+            rest_ref[...] = total[...]
 
     @pl.when(pl.program_id(0) == 0)
     def _():
@@ -308,7 +378,8 @@
     grad_query_parts = []
     for odd in range(2):
         half = slice(odd * HDIM, (odd + 1) * HDIM)
-        table[odd] = bias_table(off_ref[0, odd : odd + 1, :], length)
+        row = 2 * pl.program_id(0) + odd
+        table[odd] = bias_table(off_ref[pl.ds(row, 1), :], length)
         keys = k_ref[...] * head_lanes(odd) + key_more[odd]
         place = lane - (0 if odd else HDIM)
         value_more = ((place >= 0) & (place < 3)).astype(F32).astype(BF16)
@@ -342,18 +413,34 @@
     dq_ref[...] = jnp.concatenate(grad_query_parts, axis=0).T.astype(BF16)
 
 
-def attend_back(length_valid, offsets, qt, k, kt, v, ot, gt, lse):
+def attend_back(
+    length_valid, offsets, qt, k, kt, v, ot, gt, lse, parts, sums, axes, sizes, span
+):
     length = k.shape[0]
+    devices = sizes[0] * sizes[1]
+    link = None if devices == 1 else (axes, sizes, span)
+    rows = parts.shape[-2]
+    rest_rows = rows if link else 8
+    more = []
+    if link:
+        groups = devices // 8
+        copies = 10 + 2 * groups
+        more = reduce_scratch(groups, span[1] - span[0], rows) + [
+            pltpu.VMEM((rows, LANES), F32),
+            pltpu.VMEM((4, *sums.shape), F32),
+            pltpu.VMEM((3 + groups, *sums.shape), F32),
+            pltpu.SemaphoreType.DMA((copies,)),
+            pltpu.SemaphoreType.DMA((copies,)),
+        ]
     turned = pl.BlockSpec((LANES, length), lambda p: (p, 0))
     natural = pl.BlockSpec((length, LANES), lambda p: (0, p))
-    pair_rows = pl.BlockSpec((1, 2, 2 * length), lambda p: (p, 0, 0))
     natural_shape = jax.ShapeDtypeStruct((length, D), BF16)
     return pl.pallas_call(
-        attend_back_kernel,
+        functools.partial(attend_back_kernel, link),
         grid=(HEADS // 2,),
         in_specs=[
             pl.BlockSpec(memory_space=pltpu.SMEM),
-            pair_rows,
+            whole(offsets.shape),
             turned,
             natural,
             turned,
@@ -361,18 +448,25 @@
             turned,
             turned,
             pl.BlockSpec((1, 2, length), lambda p: (p, 0, 0)),
-        ],
-        out_specs=[natural] * 3,
-        out_shape=[natural_shape] * 3,
+            whole(parts.shape) if link else pl.BlockSpec(memory_space=pl.ANY),
+            whole(sums.shape),
+        ],
+        out_specs=[natural] * 3 + [whole((rest_rows, LANES)), whole(sums.shape)],
+        out_shape=[natural_shape] * 3
+        + [
+            jax.ShapeDtypeStruct((rest_rows, LANES), F32),
+            jax.ShapeDtypeStruct(sums.shape, F32),
+        ],
         scratch_shapes=[
             pltpu.VMEM((2, LANES, 2 * length), F32),
             pltpu.VMEM((2, length, LANES), BF16),
             pltpu.VMEM((length, length), BF16),
             pltpu.VMEM((length, length), BF16),
-        ],
-        compiler_params=params(),
+        ]
+        + more,
+        compiler_params=params(collective_id=2, has_side_effects=True) if link else params(),
         name="attend_back",
-    )(length_valid, offsets, qt, k, kt, v, ot, gt, lse)
+    )(length_valid, offsets, qt, k, kt, v, ot, gt, lse, parts, sums)
 
 
 def middle_kernel(
@@ -382,8 +476,8 @@
     cot_ref,
     gain_ref,
     w_out_ref,
-    w_in_ref,
-    w_down_ref,
+    w_in_hbm,
+    w_down_hbm,
     ar_out_ref,
     b_out_ref,
     ar_in_ref,
@@ -405,11 +499,20 @@
     sloped,
     grad_hidden,
     feeds,
+    w_in_ref,
+    w_down_ref,
+    loaded,
 ):
     step = pl.program_id(0)
+    loads = [
+        pltpu.make_async_copy(w_in_hbm, w_in_ref, loaded.at[0]),
+        pltpu.make_async_copy(w_down_hbm, w_down_ref, loaded.at[1]),
+    ]
 
     @pl.when(step == 0)
     def _():
+        for load in loads:
+            load.start()
         for ref in (
             sums_ref,
             dar_out_ref,
@@ -466,6 +569,11 @@
         activate(chunk_b, hidden_b)
         return 0
 
+    @pl.when(step == 0)
+    def _():
+        for load in loads:
+            load.wait()
+
     lax.fori_loop(0, FF // (2 * CHUNK), forward_pair, 0)
 
     packed_down = dot(active[...], ar_down_ref[...])
@@ -497,7 +605,7 @@
     rows = row_iota((MIDDLE_ROWS, 1)) + step * MIDDLE_ROWS
     valid = (rows < length_ref[0]).astype(F32)
     lane = lane_iota((8, LANES))
-    totals = jnp.zeros((8, LANES), F32)
+    totals = jnp.where((lane == 4) & (step == 0), length_ref[0].astype(F32), 0.0)
     for place, member in enumerate((inputs, branch, feed, output)):
         kept = member * valid
         totals = jnp.where(lane == place, jnp.sum(kept * kept), totals)
@@ -547,7 +655,9 @@
         middle_kernel,
         grid=(length // MIDDLE_ROWS,),
         in_specs=[pl.BlockSpec(memory_space=pltpu.SMEM), turned, tile, tile]
-        + [whole(member.shape) for member in (gain, w_out, w_in, w_down, *adapters)],
+        + [whole(gain.shape), whole(w_out.shape)]
+        + [pl.BlockSpec(memory_space=pl.ANY)] * 2
+        + [whole(member.shape) for member in adapters],
         out_specs=[tile, tile, turned] + [whole(member.shape) for member in out_shape[3:]],
         out_shape=out_shape,
         scratch_shapes=[
@@ -556,6 +666,9 @@
             pltpu.VMEM((MIDDLE_ROWS, FF), F32),
             pltpu.VMEM((MIDDLE_ROWS, FF), BF16),
             pltpu.VMEM((MIDDLE_ROWS, D), F32),
+            pltpu.VMEM(w_in.shape, BF16),
+            pltpu.VMEM(w_down.shape, BF16),
+            pltpu.SemaphoreType.DMA((2,)),
         ],
         compiler_params=params(),
         name="middle_part",
@@ -688,196 +801,253 @@
     return jnp.where(lane < LANES - shift, turned, below)[:rows]
 
 
-def narrow_to_rows(flat_ref, base, fan_in, width, place, out_ref):
-    period = 640 // width
-    groups = fan_in // period
-    lines = [flat_ref[pl.ds(base + k, groups, stride=5), :] for k in range(5)]
+GROUP = 64
+
+
+def narrow_to_rows(flat_ref, fan_in, items, out_ref):
+    groups = fan_in // GROUP
     lane = lane_iota((1, LANES))
-    for b in range(period):
-        first, shift = divmod(width * b, LANES)
-        amount = (place - shift) % LANES
-        value = lines[first] if amount == 0 else pltpu.roll(lines[first], amount, 1)
-        if shift + width > LANES:
-            value = jnp.where(
-                lane < place + LANES - shift, value, pltpu.roll(lines[first + 1], amount, 1)
-            )
-        inside = (lane >= place) & (lane < place + width)
-        out_ref[pl.ds(b, groups, stride=period), :] = jnp.where(inside, value, 0.0)
-
-
-def rows_to_narrow(in_ref, fan_in, width, place, flat_ref, base):
-    period = 640 // width
-    groups = fan_in // period
+    lines = [
+        [
+            flat_ref[pl.ds(base + k, groups, stride=width * GROUP // LANES), :]
+            for k in range(width * GROUP // LANES)
+        ]
+        for base, width, _ in items
+    ]
+    for b in range(GROUP):
+        result = jnp.zeros((groups, LANES), F32)
+        for line, (_, width, place) in zip(lines, items):
+            first, shift = divmod(width * b, LANES)
+            amount = (place - shift) % LANES
+            value = line[first] if amount == 0 else pltpu.roll(line[first], amount, 1)
+            if shift + width > LANES:
+                value = jnp.where(
+                    lane < place + LANES - shift, value, pltpu.roll(line[first + 1], amount, 1)
+                )
+            inside = (lane >= place) & (lane < place + width)
+            result = jnp.where(inside, value, result)
+        out_ref[pl.ds(b, groups, stride=GROUP), :] = result
+
+
+def rows_to_narrow(in_ref, fan_in, items, flat_ref):
+    groups = fan_in // GROUP
     lane = lane_iota((1, LANES))
-    lines = [jnp.zeros((groups, LANES), F32) for _ in range(5)]
-    for b in range(period):
-        first, shift = divmod(width * b, LANES)
-        amount = (shift - place) % LANES
-        value = in_ref[pl.ds(b, groups, stride=period), :]
-        value = value if amount == 0 else pltpu.roll(value, amount, 1)
-        inside = (lane >= shift) & (lane < shift + width)
-        lines[first] = jnp.where(inside, value, lines[first])
-        if shift + width > LANES:
-            lines[first + 1] = jnp.where(lane < shift + width - LANES, value, lines[first + 1])
-    for k in range(5):
-        flat_ref[pl.ds(base + k, groups, stride=5), :] = lines[k]
-
-
-def spread_matrix(place):
+    lines = [
+        [jnp.zeros((groups, LANES), F32) for _ in range(width * GROUP // LANES)]
+        for _, width, _ in items
+    ]
+    for b in range(GROUP):
+        source = in_ref[pl.ds(b, groups, stride=GROUP), :]
+        for line, (_, width, place) in zip(lines, items):
+            first, shift = divmod(width * b, LANES)
+            amount = (shift - place) % LANES
+            value = source if amount == 0 else pltpu.roll(source, amount, 1)
+            inside = (lane >= shift) & (lane < shift + width)
+            line[first] = jnp.where(inside, value, line[first])
+            if shift + width > LANES:
+                line[first + 1] = jnp.where(lane < shift + width - LANES, value, line[first + 1])
+    for line, (base, width, _) in zip(lines, items):
+        for k, value in enumerate(line):
+            flat_ref[pl.ds(base + k, groups, stride=width * GROUP // LANES), :] = value
+
+
+def spread_matrix(experts, source, place):
+    row = row_iota((LANES, LANES)) - source
+    lane = lane_iota((LANES, LANES)) - place
+    hit = (lane >= RANK * row) & (lane < RANK * row + RANK) & (row >= 0) & (row < experts)
+    return jnp.where(hit, 1.0, 0.0)
+
+
+def keep_matrix():
     row = row_iota((LANES, LANES))
-    lane = lane_iota((LANES, LANES)) - place
-    hit = (lane >= RANK * row) & (lane < RANK * row + RANK) & (row < EXPERTS)
-    return jnp.where(hit, 1.0, 0.0).astype(BF16)
-
-
-def unpack_kernel(
-    count,
-    shards_ref,
-    ar_qkv_ref,
-    b_qkv_ref,
-    ar_out_ref,
-    b_out_ref,
-    ar_in_ref,
-    b_in_ref,
-    ar_down_ref,
-    b_down_ref,
-    flat,
-    down,
-    router,
+    return jnp.where((row == lane_iota((LANES, LANES))) & (row < COLS), 1.0, 0.0)
+
+
+FIRST_COUNT = sum((COLS + EXPERTS) * fan_in + COLS * fan_out for fan_in, fan_out in FANS[:3])
+
+
+def unpack_ups(flat, base, fan_out, first, out_ref, column):
+    width = fan_out // LANES
+    above = jnp.zeros((first, LANES), F32)
+    below = jnp.zeros((LANES - COLS - first, LANES), F32)
+    for k in range(width):
+        part = flat[pl.ds(base + k, COLS, stride=width), :]
+        parts = [part, below] if first == 0 else [above, part, below]
+        lanes = slice(column + k * LANES, column + (k + 1) * LANES)
+        out_ref[:, lanes] = jnp.concatenate(parts, axis=0).astype(BF16)
+
+
+def unpack_first_kernel(
+    count, shards_ref, buckets_ref, table_ref, ar_ref, b_ref, off_ref, flat, down, router
 ):
-    shards = shards_ref.shape[0]
-    for index in range(shards):
+    for index in range(-(-FIRST_COUNT // count)):
         align_in(flat, shards_ref[index].astype(F32), index * count)
     starts = piece_rows()
-
-    def ups(base, fan_out, first, out_ref, column):
-        width = fan_out // LANES
-        above = jnp.zeros((first, LANES), F32)
-        below = jnp.zeros((LANES - COLS - first, LANES), F32)
-        for k in range(width):
-            part = flat[pl.ds(base + k, COLS, stride=width), :]
-            parts = [part, below] if first == 0 else [above, part, below]
-            lanes = slice(column + k * LANES, column + (k + 1) * LANES)
-            out_ref[:, lanes] = jnp.concatenate(parts, axis=0).astype(BF16)
-
-    packed = [jnp.zeros((D, LANES), F32) for _ in range(2)]
+    narrow_to_rows(flat, D, [(starts[k][0], COLS, k * COLS) for k in range(3)], down)
+    narrow_to_rows(flat, D, [(starts[k][2], EXPERTS, k * EXPERTS) for k in range(3)], router)
+    routers = router[...].astype(BF16)
+    for half in range(2):
+        matrix = spread_matrix(3 * EXPERTS, 0, 3 * COLS - half * LANES).astype(BF16)
+        packed = dot(routers, matrix)
+        packed = packed if half else packed + down[...]
+        ar_ref[:, half * LANES : (half + 1) * LANES] = packed.astype(BF16)
     for index in range(3):
-        base_a, base_b, base_r = starts[index]
-        narrow_to_rows(flat, base_a, D, COLS, index * COLS, down)
-        narrow_to_rows(flat, base_r, D, EXPERTS, 0, router)
-        packed[0] = packed[0] + down[:D]
-        for half in range(2):
-            matrix = spread_matrix((3 + index) * COLS - half * LANES)
-            packed[half] = packed[half] + dot(router[:D].astype(BF16), matrix)
-        ups(base_b, D, index * COLS, b_qkv_ref, index * D)
-    ar_qkv_ref[:, :LANES] = packed[0].astype(BF16)
-    ar_qkv_ref[:, LANES:] = packed[1].astype(BF16)
-    members = ((ar_out_ref, b_out_ref), (ar_in_ref, b_in_ref), (ar_down_ref, b_down_ref))
-    for index, (ar_ref, b_ref) in zip(range(3, 6), members):
+        unpack_ups(flat, starts[index][1], D, index * COLS, b_ref, index * D)
+    buckets = buckets_ref[...]
+    hits = jnp.where(row_iota((table_ref.shape[0], buckets.shape[1])) == buckets, LOG2E, 0.0)
+    off_ref[...] = lax.dot_general(
+        table_ref[...],
+        hits,
+        (((0,), (0,)), ((), ())),
+        preferred_element_type=F32,
+        precision=lax.Precision.HIGHEST,
+    )
+
+
+def flat_rows(count):
+    return PARAM_ROWS + shard_rows(count) + 20
+
+
+def unpack_first(shards, buckets, rel_table, count):
+    return pl.pallas_call(
+        functools.partial(unpack_first_kernel, count),
+        in_specs=[pl.BlockSpec(memory_space=pltpu.VMEM)] * 3,
+        out_specs=[pl.BlockSpec(memory_space=pltpu.VMEM)] * 3,
+        out_shape=[
+            jax.ShapeDtypeStruct((D, 2 * LANES), BF16),
+            jax.ShapeDtypeStruct((LANES, 3 * D), BF16),
+            jax.ShapeDtypeStruct((HEADS, buckets.shape[1]), F32),
+        ],
+        scratch_shapes=[
+            pltpu.VMEM((flat_rows(count), LANES), F32),
+            pltpu.VMEM((D, LANES), F32),
+            pltpu.VMEM((D, LANES), F32),
+        ],
+        compiler_params=params(),
+        name="unpack_first",
+    )(shards, buckets, rel_table)
+
+
+def unpack_rest_kernel(count, first_ref, rest_ref, *refs):
+    *outs, flat, work = refs
+    split = first_ref.shape[0]
+    for index in range(FIRST_COUNT // count, PARAM_ROWS * LANES // count):
+        shard = first_ref[index] if index < split else rest_ref[index - split]
+        align_in(flat, shard.astype(F32), index * count)
+    starts = piece_rows()
+    matrix = (keep_matrix() + spread_matrix(EXPERTS, COLS, COLS)).astype(BF16)
+    for index in range(3, 6):
         base_a, base_b, base_r = starts[index]
         fan_in, fan_out = FANS[index]
-        narrow_to_rows(flat, base_a, fan_in, COLS, 0, down)
-        narrow_to_rows(flat, base_r, fan_in, EXPERTS, 0, router)
-        wide = dot(router[:fan_in].astype(BF16), spread_matrix(COLS))
-        ar_ref[...] = (down[:fan_in] + wide).astype(BF16)
-        ups(base_b, fan_out, 0, b_ref, 0)
-
-
-def unpack(shards, count):
-    rows = shards.shape[1]
-    shapes = ((D, 2 * LANES), (LANES, 3 * D), (D, LANES), (LANES, D), (D, LANES), (LANES, FF), (FF, LANES), (LANES, D))
+        ar_ref, b_ref = outs[2 * index - 6], outs[2 * index - 5]
+        narrow_to_rows(flat, fan_in, [(base_a, COLS, 0), (base_r, EXPERTS, COLS)], work)
+        ar_ref[...] = dot(work[:fan_in].astype(BF16), matrix).astype(BF16)
+        unpack_ups(flat, base_b, fan_out, 0, b_ref, 0)
+
+
+def unpack_rest(first, rest, count):
+    shapes = [shape for fan_in, fan_out in FANS[3:] for shape in ((fan_in, LANES), (LANES, fan_out))]
     return pl.pallas_call(
-        functools.partial(unpack_kernel, count),
-        in_specs=[pl.BlockSpec(memory_space=pltpu.VMEM)],
+        functools.partial(unpack_rest_kernel, count),
+        in_specs=[pl.BlockSpec(memory_space=pltpu.VMEM)] * 2,
         out_specs=[pl.BlockSpec(memory_space=pltpu.VMEM)] * len(shapes),
         out_shape=[jax.ShapeDtypeStruct(shape, BF16) for shape in shapes],
         scratch_shapes=[
-            pltpu.VMEM((PARAM_ROWS + rows + 20, LANES), F32),
+            pltpu.VMEM((flat_rows(count), LANES), F32),
             pltpu.VMEM((FF, LANES), F32),
-            pltpu.VMEM((FF, LANES), F32),
         ],
         compiler_params=params(),
-        name="unpack",
-    )(shards)
-
-
-def gather_matrix(place):
-    row = row_iota((LANES, LANES)) - place
-    lane = lane_iota((LANES, LANES))
-    return jnp.where((row == RANK * lane) & (lane < EXPERTS), 1.0, 0.0).astype(BF16)
-
-
-def assemble_kernel(
-    count,
-    dar_qkv_ref,
-    db_qkv_ref,
-    dar_out_ref,
-    db_out_ref,
-    dar_in_ref,
-    db_in_ref,
-    dar_down_ref,
-    db_down_ref,
-    shards_ref,
-    flat,
-    down,
-    router,
-):
+        name="unpack_rest",
+    )(first, rest)
+
+
+def split_dot(value, matrix):
+    high = value.astype(BF16)
+    return dot(high, matrix) + dot((value - high.astype(F32)).astype(BF16), matrix)
+
+
+def first_of_four(experts, source, place):
+    row = row_iota((LANES, LANES)) - source
+    lane = lane_iota((LANES, LANES)) - place
+    hit = (row == RANK * lane) & (lane >= 0) & (lane < experts)
+    return jnp.where(hit, 1.0, 0.0)
+
+
+def assemble_ups(flat, base, fan_out, first, grad_ref, column):
+    width = fan_out // LANES
+    for k in range(width):
+        lanes = slice(column + k * LANES, column + (k + 1) * LANES)
+        flat[pl.ds(base + k, COLS, stride=width), :] = grad_ref[first : first + COLS, lanes]
+
+
+def assemble_rest_kernel(count, split, *refs):
+    *ins, shards_ref, more_ref, flat, work = refs
     starts = piece_rows()
-
-    def ups(base, fan_out, first, grad_ref, column):
-        width = fan_out // LANES
-        for k in range(width):
-            lanes = slice(column + k * LANES, column + (k + 1) * LANES)
-            flat[pl.ds(base + k, COLS, stride=width), :] = grad_ref[first : first + COLS, lanes]
-
-    def routers(packed, place):
-        matrix = gather_matrix(place)
-        high = packed.astype(BF16)
-        return dot(high, matrix) + dot((packed - high.astype(F32)).astype(BF16), matrix)
-
-    members = (
-        (3, dar_out_ref, db_out_ref),
-        (4, dar_in_ref, db_in_ref),
-        (5, dar_down_ref, db_down_ref),
-    )
-    for index, dar_ref, db_ref in members:
+    matrix = (keep_matrix() + first_of_four(EXPERTS, COLS, COLS)).astype(BF16)
+    for index in range(3, 6):
         base_a, base_b, base_r = starts[index]
         fan_in, fan_out = FANS[index]
-        packed = pad_rows(dar_ref[...], LANES).T
-        down[:fan_in] = packed
-        rows_to_narrow(down, fan_in, COLS, 0, flat, base_a)
-        router[:fan_in] = routers(packed, COLS)
-        rows_to_narrow(router, fan_in, EXPERTS, 0, flat, base_r)
-        ups(base_b, fan_out, 0, db_ref, 0)
-    down[:D] = dar_qkv_ref[:LANES].T
+        dar_ref, db_ref = ins[2 * index - 6], ins[2 * index - 5]
+        work[:fan_in] = split_dot(pad_rows(dar_ref[...], LANES).T, matrix)
+        rows_to_narrow(work, fan_in, [(base_a, COLS, 0), (base_r, EXPERTS, COLS)], flat)
+        assemble_ups(flat, base_b, fan_out, 0, db_ref, 0)
+    for index in range(shards_ref.shape[0]):
+        shards_ref[index] = align_out(flat, shards_ref.shape[1], (split + index) * count)
+    begin = FIRST_COUNT // LANES
+    more_ref[...] = flat[begin : begin + more_ref.shape[0]]
+
+
+def assemble_rest(grads, devices, split, count):
+    rows = shard_rows(count)
+    more = (split * count - FIRST_COUNT) // (8 * LANES) * 8 + 16
+    return pl.pallas_call(
+        functools.partial(assemble_rest_kernel, count, split),
+        in_specs=[pl.BlockSpec(memory_space=pltpu.VMEM)] * len(grads),
+        out_specs=[pl.BlockSpec(memory_space=pltpu.VMEM)] * 2,
+        out_shape=[
+            jax.ShapeDtypeStruct((max(devices - split, 1), rows, LANES), F32),
+            jax.ShapeDtypeStruct((more, LANES), F32),
+        ],
+        scratch_shapes=[
+            pltpu.VMEM((flat_rows(count), LANES), F32),
+            pltpu.VMEM((FF, LANES), F32),
+        ],
+        compiler_params=params(),
+        name="assemble_rest",
+    )(*grads)
+
+
+def assemble_first_kernel(count, dar_ref, db_ref, more_ref, shards_ref, flat, down, router):
+    starts = piece_rows()
+    down[...] = dar_ref[:LANES].T
+    rows_to_narrow(down, D, [(starts[k][0], COLS, k * COLS) for k in range(3)], flat)
     first_router = 3 * COLS
-    packed_router = dar_qkv_ref[first_router : first_router + LANES].T
+    turned = dar_ref[first_router : first_router + LANES].T
+    router[...] = split_dot(turned, first_of_four(3 * EXPERTS, 0, 0).astype(BF16))
+    rows_to_narrow(router, D, [(starts[k][2], EXPERTS, k * EXPERTS) for k in range(3)], flat)
     for index in range(3):
-        base_a, base_b, base_r = starts[index]
-        rows_to_narrow(down, D, COLS, index * COLS, flat, base_a)
-        router[:D] = routers(packed_router, index * COLS)
-        rows_to_narrow(router, D, EXPERTS, 0, flat, base_r)
-        ups(base_b, D, index * COLS, db_qkv_ref, index * D)
-    shards, rows = shards_ref.shape[0], shards_ref.shape[1]
-    for index in range(shards):
-        shards_ref[index] = align_out(flat, rows, index * count)
-
-
-def assemble(grads, shards, count):
+        assemble_ups(flat, starts[index][1], D, index * COLS, db_ref, index * D)
+    begin = FIRST_COUNT // LANES
+    flat[begin : begin + more_ref.shape[0]] = more_ref[...]
+    for index in range(shards_ref.shape[0]):
+        shards_ref[index] = align_out(flat, shards_ref.shape[1], index * count)
+
+
+def assemble_first(dar, db, more, split, count):
     rows = shard_rows(count)
     return pl.pallas_call(
-        functools.partial(assemble_kernel, count),
-        in_specs=[pl.BlockSpec(memory_space=pltpu.VMEM)] * len(grads),
+        functools.partial(assemble_first_kernel, count),
+        in_specs=[pl.BlockSpec(memory_space=pltpu.VMEM)] * 3,
         out_specs=pl.BlockSpec(memory_space=pltpu.VMEM),
-        out_shape=jax.ShapeDtypeStruct((shards, rows, LANES), F32),
+        out_shape=jax.ShapeDtypeStruct((split, rows, LANES), F32),
         scratch_shapes=[
-            pltpu.VMEM((PARAM_ROWS + rows + 20, LANES), F32),
-            pltpu.VMEM((FF, LANES), F32),
-            pltpu.VMEM((FF, LANES), F32),
+            pltpu.VMEM((flat_rows(count), LANES), F32),
+            pltpu.VMEM((D, LANES), F32),
+            pltpu.VMEM((D, LANES), F32),
         ],
         compiler_params=params(),
-        name="assemble",
-    )(*grads)
+        name="assemble_first",
+    )(dar, db, more)
 
 
 MESH = pl.DeviceIdType.MESH
@@ -913,195 +1083,334 @@
     pl.semaphore_wait(barrier, len(peers))
 
 
-def gather_kernel(axes, sizes, shard_ref, out_ref, send, receive, local):
-    me, coordinates = place_of(axes, sizes)
-    groups = out_ref.shape[0]
-    group = me // 8
-    low, first, second, both, other, over_x, over_y = partners_of(me)
-
-    def device(group_index, low_index):
-        return coordinates(group_index * 8 + low_index)
-
-    others = [(group + step) % groups for step in range(1, groups)]
-    peers = [device(index, low) for index in others]
-    peers += [device(group, partner) for partner in (first, second, low + other)]
-    greet(peers)
-    counter = [0]
-
-    def start(source, target, peer):
-        index = counter[0]
-        counter[0] += 1
-        copy = pltpu.make_async_remote_copy(
+class Ring:
+    def __init__(self, axes, sizes, send, receive):
+        self.me, self.coordinates = place_of(axes, sizes)
+        self.groups = sizes[0] * sizes[1] // 8
+        self.group = self.me // 8
+        places = partners_of(self.me)
+        self.low, self.first, self.second, self.both, self.other, self.over_x, self.over_y = places
+        self.mate = self.low + self.other
+        self.send, self.receive = send, receive
+        self.copies = {}
+
+    def device(self, group, low):
+        return self.coordinates(group * 8 + low)
+
+    def greet(self):
+        peers = [
+            self.device((self.group + step) % self.groups, self.low)
+            for step in range(1, self.groups)
+        ]
+        peers += [self.device(self.group, low) for low in (self.first, self.second, self.mate)]
+        greet(peers)
+
+    def copy(self, slot, source, target, peer, arrival=None):
+        return pltpu.make_async_remote_copy(
             src_ref=source,
             dst_ref=target,
-            send_sem=send.at[index],
-            recv_sem=receive.at[index],
+            send_sem=self.send.at[slot],
+            recv_sem=self.receive.at[slot if arrival is None else arrival],
             device_id=peer,
             device_id_type=MESH,
         )
-        copy.start()
-        return copy
-
-    own = pltpu.make_async_copy(shard_ref, out_ref.at[group, low], local)
-    own.start()
-    around = [start(shard_ref, out_ref.at[group, low], device(index, low)) for index in others]
-    own.wait()
-    for copy in around:
-        copy.wait()
-
-    def push(part, partner):
-        return start(out_ref.at[:, part], out_ref.at[:, part], device(group, partner))
-
-    one = push(low, first)
-    two = push(low, second)
-    core_own = push(low, low + other)
-    one.wait()
-    three = push(first, second)
-    core_first = push(first, low + other)
-    two.wait()
-    core_second = push(second, low + other)
-    three.wait()
-    core_both = push(both, low + other)
-    for copy in (core_own, core_first, core_second, core_both):
-        copy.wait()
-
-
-def gather(shard, axes, sizes):
+
+
+def gather_phases(ring, span, shard_ref, out_ref, local):
+    begin, end = span
+    base = ring.groups
+    inside = (ring.group >= begin) & (ring.group < end)
+
+    def around(step):
+        target = (ring.group + step) % ring.groups
+        return ring.copy(
+            step,
+            shard_ref,
+            out_ref.at[ring.group - begin, ring.low],
+            ring.device(target, ring.low),
+            base + 7 + ring.group,
+        )
+
+    def arrived(group):
+        return ring.copy(
+            0,
+            shard_ref,
+            out_ref.at[group - begin, ring.low],
+            ring.device(group, ring.low),
+            base + 7 + group,
+        )
+
+    def push(slot, part, partner):
+        return ring.copy(
+            base + slot, out_ref.at[:, part], out_ref.at[:, part], ring.device(ring.group, partner)
+        )
+
+    one = push(0, ring.low, ring.first)
+    two = push(1, ring.low, ring.second)
+    three = push(2, ring.first, ring.second)
+    cores = [
+        push(3 + index, part, ring.mate)
+        for index, part in enumerate((ring.low, ring.first, ring.second, ring.both))
+    ]
+
+    def own():
+        return pltpu.make_async_copy(
+            shard_ref, out_ref.at[ring.group - begin, ring.low], local
+        )
+
+    def phase0():
+        ring.greet()
+
+        @pl.when(inside)
+        def _():
+            own().start()
+            for step in range(1, ring.groups):
+                around(step).start()
+
+    def phase1():
+        @pl.when(inside)
+        def _():
+            own().wait()
+            for step in range(1, ring.groups):
+                around(step).wait_send()
+
+        for group in range(begin, end):
+
+            @pl.when(ring.group != group)
+            def _():
+                arrived(group).wait_recv()
+
+        for copy in (one, two, cores[0]):
+            copy.start()
+
+    def phase2():
+        one.wait()
+        three.start()
+        cores[1].start()
+
+    def phase3():
+        two.wait()
+        cores[2].start()
+        three.wait()
+        cores[3].start()
+
+    def phase4():
+        for copy in cores:
+            copy.wait()
+
+    return phase0, phase1, phase2, phase3, phase4
+
+
+def gather_semaphores(groups):
+    return [
+        pltpu.SemaphoreType.DMA((groups + 7,)),
+        pltpu.SemaphoreType.DMA((2 * groups + 7,)),
+        pltpu.SemaphoreType.DMA,
+    ]
+
+
+def gather_kernel(axes, sizes, span, shard_ref, out_ref, send, receive, local):
+    for phase in gather_phases(Ring(axes, sizes, send, receive), span, shard_ref, out_ref, local):
+        phase()
+
+
+def gather(shard, axes, sizes, span):
     groups = sizes[0] * sizes[1] // 8
-    copies = groups - 1 + 7
     return pl.pallas_call(
-        functools.partial(gather_kernel, axes, sizes),
+        functools.partial(gather_kernel, axes, sizes, span),
         in_specs=[pl.BlockSpec(memory_space=pltpu.VMEM)],
         out_specs=pl.BlockSpec(memory_space=pltpu.VMEM),
-        out_shape=jax.ShapeDtypeStruct((groups, 8, *shard.shape), shard.dtype),
-        scratch_shapes=[
-            pltpu.SemaphoreType.DMA((copies,)),
-            pltpu.SemaphoreType.DMA((copies,)),
-            pltpu.SemaphoreType.DMA,
-        ],
+        out_shape=jax.ShapeDtypeStruct((span[1] - span[0], 8, *shard.shape), shard.dtype),
+        scratch_shapes=gather_semaphores(groups),
         compiler_params=params(collective_id=0, has_side_effects=True),
         name="gather",
     )(shard)
 
 
-def reduce_kernel(
-    axes, sizes, parts_ref, sums_ref, out_ref, total_ref, outbox, inbox, near_out, near_in, far_in, own, send, receive
-):
-    me, coordinates = place_of(axes, sizes)
-    groups = parts_ref.shape[0]
-    group = me // 8
-    low, first, second, both, other, over_x, over_y = partners_of(me)
-
-    def device(group_index, low_index):
-        return coordinates(group_index * 8 + low_index)
-
-    others = [(group + step) % groups for step in range(1, groups)]
-    peers = [device(index, low) for index in others]
-    peers += [device(group, partner) for partner in (first, second, low + other)]
-    greet(peers)
-    counter = [0]
-
-    def start(source, target, peer):
-        index = counter[0]
-        counter[0] += 1
-        copy = pltpu.make_async_remote_copy(
-            src_ref=source,
-            dst_ref=target,
-            send_sem=send.at[index],
-            recv_sem=receive.at[index],
-            device_id=peer,
-            device_id_type=MESH,
+def reduce_phases(ring, span, parts_ref, boxes, sums_ref=None, sum_boxes=None):
+    begin, end = span
+    outbox, inbox, half, own, far_out, far_in, out_ref = boxes
+    groups = ring.groups
+    inside = (ring.group >= begin) & (ring.group < end)
+    core_parts = (ring.first, ring.both, ring.second, ring.low)
+    near = [ring.mate] * 4 + [ring.second, ring.second, ring.first]
+
+    def push(slot):
+        return ring.copy(slot, outbox.at[slot], inbox.at[slot], ring.device(ring.group, near[slot]))
+
+    def fill(slot, value):
+        outbox[slot] = value.astype(BF16)
+        push(slot).start()
+
+    def around(group):
+        return ring.copy(
+            7 + group - begin,
+            far_out.at[group - begin],
+            far_in.at[ring.group],
+            ring.device(group, ring.low),
+            7 + ring.group,
         )
-        copy.start()
-        return copy
-
-    def push(slot, value, partner):
-        outbox[slot] = value.astype(BF16)
-        return start(outbox.at[slot], inbox.at[slot], device(group, partner))
-
-    def push_sums(slot, value, partner):
-        near_out[slot] = value
-        return start(near_out.at[slot], near_in.at[slot], device(group, partner))
-
-    mate = low + other
-    sums = sums_ref[...]
-    sums_core = push_sums(0, sums, mate)
-    core = [
-        push(slot, parts_ref[:, part + other], mate)
-        for slot, part in enumerate((first, both, second, low))
+
+    def arrived(group):
+        return ring.copy(
+            7,
+            far_out.at[0],
+            far_in.at[group],
+            ring.device(group, ring.low),
+            7 + group,
+        )
+
+    base = 7 + groups
+    sum_peers = (ring.mate, ring.over_x, ring.over_y)
+
+    def push_sums(slot):
+        near_out, near_in = sum_boxes
+        return ring.copy(
+            base + slot,
+            near_out.at[slot],
+            near_in.at[slot],
+            ring.device(ring.group, sum_peers[slot]),
+        )
+
+    def around_sums(step):
+        near_out, near_in = sum_boxes
+        target = (ring.group + step) % groups
+        return ring.copy(
+            base + 2 + step,
+            near_out.at[3],
+            near_in.at[3 + ring.group],
+            ring.device(target, ring.low),
+        )
+
+    def start_sums(slot, value):
+        if sum_boxes is not None:
+            sum_boxes[0][slot] = value
+            push_sums(slot).start()
+
+    def phase0():
+        ring.greet()
+        if sum_boxes is not None:
+            start_sums(0, sums_ref[...])
+        for slot, part in enumerate(core_parts):
+            fill(slot, parts_ref[:, part + ring.other])
+
+    def phase1():
+        push(0).wait()
+        fill(4, parts_ref[:, ring.second] + inbox[0].astype(F32))
+        push(1).wait()
+        fill(5, parts_ref[:, ring.both] + inbox[1].astype(F32))
+        if sum_boxes is not None:
+            push_sums(0).wait()
+            start_sums(1, sum_boxes[0][0] + sum_boxes[1][0])
+        push(2).wait()
+        half[...] = parts_ref[:, ring.first] + inbox[2].astype(F32)
+        push(3).wait()
+        own[...] = parts_ref[:, ring.low] + inbox[3].astype(F32)
+
+    def phase2():
+        push(5).wait()
+        fill(6, half[...] + inbox[5].astype(F32))
+        if sum_boxes is not None:
+            push_sums(1).wait()
+            start_sums(2, sum_boxes[0][1] + sum_boxes[1][1])
+        push(4).wait()
+        own[...] = own[...] + inbox[4].astype(F32)
+
+    def phase3():
+        push(6).wait()
+        own[...] = own[...] + inbox[6].astype(F32)
+        far_out[...] = own[...].astype(BF16)
+        for group in range(begin, end):
+
+            @pl.when(ring.group != group)
+            def _():
+                around(group).start()
+
+        if sum_boxes is not None:
+            near_out, near_in = sum_boxes
+            push_sums(2).wait()
+            near_out[3] = near_out[2] + near_in[2]
+            for step in range(1, groups):
+                around_sums(step).start()
+            near_in[3 + ring.group] = near_out[3]
+
+    def phase4(finish_sums=None):
+        for group in range(begin, end):
+
+            @pl.when(ring.group != group)
+            def _():
+                around(group).wait_send()
+
+        @pl.when(inside)
+        def _():
+            for group in range(groups):
+
+                @pl.when(ring.group != group)
+                def _():
+                    arrived(group).wait_recv()
+
+            total = own[ring.group - begin]
+            for step in range(1, groups):
+                total = total + far_in[(ring.group + step) % groups].astype(F32)
+            out_ref[...] = total
+
+        if sum_boxes is not None:
+            near_out, near_in = sum_boxes
+            for step in range(1, groups):
+                around_sums(step).wait()
+            whole_sum = near_in[3]
+            for index in range(1, groups):
+                whole_sum = whole_sum + near_in[3 + index]
+            finish_sums(whole_sum)
+
+    return phase0, phase1, phase2, phase3, phase4
+
+
+def reduce_scratch(groups, count, rows):
+    return [
+        pltpu.VMEM((7, count, rows, LANES), BF16),
+        pltpu.VMEM((7, count, rows, LANES), BF16),
+        pltpu.VMEM((count, rows, LANES), F32),
+        pltpu.VMEM((count, rows, LANES), F32),
+        pltpu.VMEM((count, rows, LANES), BF16),
+        pltpu.VMEM((groups, rows, LANES), BF16),
     ]
-    core[0].wait()
-    half_second = parts_ref[:, second] + inbox[0].astype(F32)
-    to_second = push(4, half_second, second)
-    core[1].wait()
-    half_both = parts_ref[:, both] + inbox[1].astype(F32)
-    to_both = push(5, half_both, second)
-    sums_core.wait()
-    sums = sums + near_in[0]
-    sums_x = push_sums(1, sums, over_x)
-    core[2].wait()
-    half_first = parts_ref[:, first] + inbox[2].astype(F32)
-    core[3].wait()
-    half_low = parts_ref[:, low] + inbox[3].astype(F32)
-    to_both.wait()
-    quarter_first = half_first + inbox[5].astype(F32)
-    to_first = push(6, quarter_first, first)
-    sums_x.wait()
-    sums = sums + near_in[1]
-    sums_y = push_sums(2, sums, over_y)
-    to_second.wait()
-    half_low = half_low + inbox[4].astype(F32)
-    to_first.wait()
-    own[...] = half_low + inbox[6].astype(F32)
-    outbox[7] = own[...].astype(BF16)
-    around = [
-        start(outbox.at[7, index], far_in.at[step], device(index, low))
-        for step, index in enumerate(others)
-    ]
-    sums_y.wait()
-    near_out[3] = sums + near_in[2]
-    around_sums = [
-        start(near_out.at[3], near_in.at[4 + group], device(index, low))
-        for index in others
-    ]
-    near_in[4 + group] = near_out[3]
-    total = own[group]
-    for step, copy in enumerate(around):
-        copy.wait()
-        total = total + far_in[step].astype(F32)
-    out_ref[...] = total
-    for copy in around_sums:
-        copy.wait()
-    whole_sum = near_in[4]
-    for index in range(1, groups):
-        whole_sum = whole_sum + near_in[4 + index]
-    total_ref[...] = whole_sum
-
-
-def reduce_scatter(parts, sums, axes, sizes):
-    groups, _, rows, lanes = parts.shape
-    copies = 7 + 3 + 2 * (groups - 1)
+
+
+def reduce_kernel(axes, sizes, span, parts_ref, rest_ref, out_ref, *scratch):
+    *boxes, total, send, receive = scratch
+    ring = Ring(axes, sizes, send, receive)
+    for phase in reduce_phases(ring, span, parts_ref, (*boxes, total)):
+        phase()
+    first = (ring.group >= span[0]) & (ring.group < span[1])
+
+    @pl.when(first)
+    def _():
+        out_ref[...] = total[...]
+
+    @pl.when(jnp.logical_not(first))
+    def _():
+        out_ref[...] = rest_ref[...]
+
+
+def reduce_scatter(parts, rest, axes, sizes, span):
+    count, _, rows, lanes = parts.shape
+    groups = sizes[0] * sizes[1] // 8
+    copies = 7 + groups
     return pl.pallas_call(
-        functools.partial(reduce_kernel, axes, sizes),
+        functools.partial(reduce_kernel, axes, sizes, span),
         in_specs=[pl.BlockSpec(memory_space=pltpu.VMEM)] * 2,
-        out_specs=[pl.BlockSpec(memory_space=pltpu.VMEM)] * 2,
-        out_shape=[
-            jax.ShapeDtypeStruct((rows, lanes), F32),
-            jax.ShapeDtypeStruct(sums.shape, F32),
-        ],
-        scratch_shapes=[
-            pltpu.VMEM((8, groups, rows, lanes), BF16),
-            pltpu.VMEM((7, groups, rows, lanes), BF16),
-            pltpu.VMEM((4, *sums.shape), F32),
-            pltpu.VMEM((4 + groups, *sums.shape), F32),
-            pltpu.VMEM((groups - 1, rows, lanes), BF16),
-            pltpu.VMEM((groups, rows, lanes), F32),
+        out_specs=pl.BlockSpec(memory_space=pltpu.VMEM),
+        out_shape=jax.ShapeDtypeStruct((rows, lanes), F32),
+        scratch_shapes=reduce_scratch(groups, count, rows)
+        + [
+            pltpu.VMEM((rows, lanes), F32),
             pltpu.SemaphoreType.DMA((copies,)),
             pltpu.SemaphoreType.DMA((copies,)),
         ],
-        compiler_params=params(collective_id=1, has_side_effects=True),
+        compiler_params=params(collective_id=3, has_side_effects=True),
         name="reduce_scatter",
-    )(parts, sums)
+    )(parts, rest)
 
 
 def per_device(
@@ -1123,42 +1432,49 @@
     seq_count, length, width = tokens.shape
     x = tokens.reshape(length, width)
     cot = cotangent.reshape(length, width)
+    gain_first = gain_attn.reshape(1, width)
+    gain_second = gain_ff.reshape(1, width)
     devices = sizes[0] * sizes[1]
     count = adapters.shape[0]
     rows = shard_rows(count)
     shard = jnp.pad(adapters, (0, rows * LANES - count)).reshape(rows, LANES)
+    groups = devices // 8
+    split_groups = min(-(-FIRST_COUNT // (8 * count)), max(groups - 1, 1))
+    split = min(8 * split_groups, devices)
+    first_span, rest_span = (0, split_groups), (split_groups, groups)
     if devices == 1:
-        shards = shard[None]
+        first = shard[None]
     else:
-        shards = gather(shard, axes, sizes).reshape(devices, rows, LANES)
-    ar_qkv, b_qkv, *rest = unpack(shards, count)
-    gain_first = gain_attn.reshape(1, width)
-    gain_second = gain_ff.reshape(1, width)
-
-    reversed_buckets = jnp.pad(buckets[::-1], (0, 1))
-    hits = (jnp.arange(rel_table.shape[0])[:, None] == reversed_buckets[None, :]).astype(F32)
-    offsets = jnp.dot(rel_table.T * LOG2E, hits, precision=lax.Precision.HIGHEST)
-    offsets = offsets.reshape(HEADS // 2, 2, 2 * length)
-
-    qt, k, kt, v, vt, zg = project(x, gain_first, w_qkv, ar_qkv, b_qkv)
+        first = gather(shard, axes, sizes, first_span).reshape(split, rows, LANES)
+    reversed_buckets = jnp.pad(buckets[::-1], (0, 1)).reshape(1, 2 * length)
+    ar_qkv, b_qkv, offsets = unpack_first(first, reversed_buckets, rel_table, count)
+    qt, k, kt, v, vt, zg, rest = project(
+        x, gain_first, w_qkv, ar_qkv, b_qkv, shard, axes, sizes, rest_span
+    )
+    rest = rest.reshape(-1, *rest.shape[2:])
     ot, lse = attend(lengths, offsets, qt, k, vt)
+    packed = unpack_rest(first, rest, count)
     block_out, dmid, gt, sums, *grads = middle_part(
-        lengths, ot, x, cot, gain_second, w_out, w_in, w_down, rest
+        lengths, ot, x, cot, gain_second, w_out, w_in, w_down, packed
     )
-    dq, dk, dv = attend_back(lengths, offsets, qt, k, kt, v, ot, gt, lse)
+    parts, more = assemble_rest(grads, devices, split, count)
+    if devices > 1:
+        parts = parts.reshape(groups - split_groups, 8, rows, LANES)
+    dq, dk, dv, rest_sum, roots = attend_back(
+        lengths, offsets, qt, k, kt, v, ot, gt, lse, parts, sums, axes, sizes, rest_span
+    )
     tokens_grad, dar_qkv, db_qkv = project_back(
         x, gain_first, w_qkv, ar_qkv, b_qkv, zg, dq, dk, dv, dmid
     )
 
-    parts = assemble((dar_qkv, db_qkv, *grads), devices, count)
-    sums = jnp.where(jnp.arange(LANES)[None, :] == 4, jnp.sum(lengths).astype(F32), sums)
+    parts = assemble_first(dar_qkv, db_qkv, more, split, count)
     if devices == 1:
-        mine, sums = parts[0], sums
+        mine = parts[0]
     else:
-        parts = parts.reshape(devices // 8, 8, rows, LANES)
-        mine, sums = reduce_scatter(parts, sums, axes, sizes)
+        parts = parts.reshape(split_groups, 8, rows, LANES)
+        mine = reduce_scatter(parts, rest_sum, axes, sizes, first_span)
     grad_shard = mine.reshape(-1)[:count]
-    root_squares = jnp.sqrt(sums[0, :4] / (sums[0, 4] * width))
+    root_squares = roots[0, :4]
     return (
         block_out.reshape(tokens.shape),
         tokens_grad.reshape(tokens.shape),

time: 208 us -> 212 us (1.019)
  Pallas kernels: 195 us -> 200 us
    pallas_call x6 -> x8, Pallas kernels: 108 us -> 115 us  [the longest x1 38.7 us: attend_back(): pl.pallas_call(functools.partial(attend_back_kernel, link), grid=(HEADS /...]
where the time goes in v1:
time: 212 us; the launch traced here: 211 us
  Pallas kernels  200 us (94%)
  local copies, waits for them, and re-layouts  9.49 us (4%)
    pallas_call x1, Pallas kernels, middle_part(): pl.pallas_call(middle_kernel, grid=(length // MIDDLE_ROWS,), in_specs=[pl...  52.6 us
    pallas_call x1, Pallas kernels, attend_back(): pl.pallas_call(functools.partial(attend_back_kernel, link), grid=(HEADS /...  38.7 us
    pallas_call x1, Pallas kernels, project(): pl.pallas_call(functools.partial(project_kernel, link), grid=(length // R...  21.3 us
    pallas_call x1, Pallas kernels, attend(): pl.pallas_call(attend_kernel, grid=(HEADS // 2,), in_specs=[pl.BlockSpec(...  19.7 us
    pallas_call x1, Pallas kernels, gather(): pl.pallas_call(functools.partial(gather_kernel, axes, sizes, span), in_sp...  18.9 us
    pallas_call x1, Pallas kernels, reduce_scatter(): pl.pallas_call(functools.partial(reduce_kernel, axes, sizes, span), in_sp...  16.8 us
    pallas_call x1, Pallas kernels, project_back(): pl.pallas_call(project_back_kernel, grid=(length // ROWS,), in_specs=[til...  12.6 us
    pallas_call x1, Pallas kernels, assemble_rest(): pl.pallas_call(functools.partial(assemble_rest_kernel, count, split), in_...  6.1 us

profile of v1, /device:TPU:0, one launch (start us, length us, event | category | flops | bytes accessed | tf_op | source)
XLA Modules:
  0.0 210.9 jit_solution(1918109625273010834)
XLA Ops:
  1.3 1.3 reshape.51.gain_ref
  2.6 1.3 reshape.53.gain_ref
  3.8 0.8 reverse
  4.6 0.1 slice.10
  4.7 0.6 pad.9
  5.3 1.4 copy.16.table_ref
  6.7 1.4 pad_bitcast_fusion.shard_ref
  8.1 18.9 %gather.1 = bf16[2,8,160,128]{3,2,1,0:T(8,128)(2,1)} custom-call(bf16[160,128]{1,0:T(8,128)(2,1)} %pad_bitcast_fusion.shard_ref), custom_call_target="tpu_custom_call" | custom-call | tf_op jit(solution)/shard_map/gather/pallas_call | solution.py:1219
  27.0 3.5 %unpack_first.1 = (bf16[768,256]{1,0:T(8,128)(2,1)}, bf16[128,2304]{1,0:T(8,128)(2,1)}, f32[12,2048]{1,0:T(8,128)}) custom-call(bf16[16,160,128]{2,1,0:T(8,128)(2,1)} %bitcast.18, s32[1,2048]{1,0:T(1,128)} %bitcast.25, f32[32,12]{1,0:T(8,128)} %copy.16.table_ref), custom_call_target="tpu_custom_call" | custom-call | tf_op jit(solution)/shard_map/unpack_first/pallas_call | solution.py:912
  30.5 21.3 %project.1 = (bf16[768,1024]{1,0:T(8,128)(2,1)}, bf16[1024,768]{1,0:T(8,128)(2,1)}, bf16[768,1024]{1,0:T(8,128)(2,1)}, bf16[1024,768]{1,0:T(8,128)(2,1)}, bf16[7...) custom-call(bf16[160,128]{1,0:T(8,128)(2,1)} %pad_bitcast_fusion.shard_ref, ...), custom_call_target="tpu_custom_call" | custom-call | tf_op jit(solution)/shard_map/project/pallas_call | solution.py:181
  51.9 19.7 %attend.1 = (bf16[768,1024]{1,0:T(8,128)(2,1)}, f32[6,2,1024]{2,1,0:T(2,128)}) custom-call(s32[1]{0:T(128)S(6)} %copy.17.length_ref, f32[12,2048]{1,0:T(8,128)} %get-tuple-element.42.off_ref, bf16[768,1024]{1,0:T(8,128)(2,1)} %get-tuple-element.45.qt_ref, bf16[1024,768]{1,0:T(8,128)(2,1)} %get-tuple-element.46.k_ref, bf16[768,1024]{1,0:T(8,128)(2,1)} %get-tuple-element.47.vt_ref), custom_call_target="tpu_custom_call" | custom-call | tf_op jit(solution)/shard_map/attend/pallas_call | solution.py:300
  71.6 5.7 %unpack_rest.1 = (bf16[768,128]{1,0:T(8,128)(2,1)}, bf16[128,768]{1,0:T(8,128)(2,1)}, bf16[768,128]{1,0:T(8,128)(2,1)}, bf16[128,3072]{1,0:T(8,128)(2,1)}, bf16[...) custom-call(bf16[16,160,128]{2,1,0:T(8,128)(2,1)} %bitcast.19, bf16[16,160,128]{2,1,0:T(8,128)(2,1)} %bitcast.23), custom_call_target="tpu_custom_call" | custom-call | tf_op jit(solution)/shard_map/unpack_rest/pallas_call | solution.py:950
  77.2 52.6 %middle_part.1 = (bf16[1024,768]{1,0:T(8,128)(2,1)}, f32[1024,768]{1,0:T(8,128)}, bf16[768,1024]{1,0:T(8,128)(2,1)}, f32[8,128]{1,0:T(8,128)}, f32[80,768]{1,0:T...) custom-call(s32[1]{0:T(128)S(6)} %copy.17.length_ref, ...), custom_call_target="tpu_custom_call" | custom-call | tf_op jit(solution)/shard_map/middle_part/pallas_call | solution.py:654
  129.9 6.1 %assemble_rest.1 = (f32[16,160,128]{2,1,0:T(8,128)}, f32[824,128]{1,0:T(8,128)}) custom-call(f32[80,768]{1,0:T(8,128)} %get-tuple-element.62.refs_0_, f32[48,768]{1,0:T(8,128)} %get-tuple-element.63.refs_1_, f32[80,768]{1,0:T(8,128)} %get-tuple-element.64.refs_2_, f32[48,3072]{1,0:T(8,128)} %get-tuple-element.65.refs_3_, ...), custom_call_target="tpu_custom_call" | custom-call | tf_op jit(solution)/shard_map/assemble_rest/pallas_call | solution.py:1003
  136.0 38.7 %attend_back.1 = (bf16[1024,768]{1,0:T(8,128)(2,1)}, bf16[1024,768]{1,0:T(8,128)(2,1)}, bf16[1024,768]{1,0:T(8,128)(2,1)}, f32[160,128]{1,0:T(8,128)}, f32[8,128]{1,0:T(8,128)}) custom-call(s32[1]{0:T(128)S(6)} %copy.17.length_ref, f32[12,2048]{1,0:T(8,128)} %get-tuple-element.42.off_ref, bf16[768,1024]{1,0:T(8,128)(2,1)} %get-tuple-element.45.qt_ref, ...), custom_call_target="tpu_custom_call" | custom-call | tf_op jit(solution)/shard_map/attend_back/pallas_call | solution.py:438
  174.7 12.6 %project_back.1 = (f32[1024,768]{1,0:T(8,128)}, f32[256,768]{1,0:T(8,128)}, f32[128,2304]{1,0:T(8,128)}) custom-call(bf16[1024,768]{1,0:T(8,128)(2,1)} %bitcast.17, f32[1,768]{1,0:T(1,128)} %reshape.51.gain_ref, bf16[768,2304]{1,0:T(8,128)(2,1)} %w_ref.3, bf16[768,256]{1,0:T(8,128)(2,1)} %get-tuple-element.43.ar_ref, ...), custom_call_target="tpu_custom_call" | custom-call | tf_op jit(solution)/shard_map/project_back/pallas_call | solution.py:734
  187.3 1.2 slice_bitcast_fusion
  188.5 4.1 %assemble_first.1 = f32[16,160,128]{2,1,0:T(8,128)} custom-call(f32[256,768]{1,0:T(8,128)} %get-tuple-element.75.dar_ref, f32[128,2304]{1,0:T(8,128)} %get-tuple-element.76.db_ref, f32[824,128]{1,0:T(8,128)} %get-tuple-element.77.more_ref), custom_call_target="tpu_custom_call" | custom-call | tf_op jit(solution)/shard_map/assemble_first/pallas_call | solution.py:1038
  192.6 16.8 %reduce_scatter.1 = f32[160,128]{1,0:T(8,128)} custom-call(f32[2,8,160,128]{3,2,1,0:T(8,128)} %bitcast.20, f32[160,128]{1,0:T(8,128)} %get-tuple-element.78.rest_ref), custom_call_target="tpu_custom_call" | custom-call | tf_op jit(solution)/shard_map/reduce_scatter/pallas_call | solution.py:1400
  209.4 1.5 slice.8

commit v2 on v1

--- a/solution.py
+++ b/solution.py
@@ -108,111 +108,6 @@
 def whole(shape):
     zeros = (0,) * len(shape)
     return pl.BlockSpec(shape, lambda *_: zeros, pipeline_mode=pl.Buffered(1))
-
-
-def project_kernel(
-    link,
-    shard_ref,
-    x_ref,
-    gain_ref,
-    w_ref,
-    ar_ref,
-    b_ref,
-    qt_ref,
-    k_ref,
-    kt_ref,
-    v_ref,
-    vt_ref,
-    zg_ref,
-    shards_ref,
-    landing,
-    send,
-    receive,
-    local,
-):
-    step = pl.program_id(0)
-    if link is not None:
-        axes, sizes, span = link
-        ring = Ring(axes, sizes, send, receive)
-        phases = gather_phases(ring, span, shard_ref, landing, local)
-        for turn, phase in enumerate(phases[:4]):
-            pl.when(step == turn)(phase)
-    values = x_ref[...].astype(F32)
-    normed = (values * rms_inverse(values) * gain_ref[...]).astype(BF16)
-    packed = dot(normed, ar_ref[...]).T
-    lowrank = packed[: 3 * COLS]
-    gates = jnp.concatenate(
-        [gates_of(packed[first : first + COLS]) for first in range(3 * COLS, 6 * COLS, COLS)], axis=0
-    )
-    zg_ref[: 3 * COLS] = lowrank
-    zg_ref[3 * COLS :] = gates
-    mixed = pad_rows(lowrank * gates, LANES).astype(BF16).T
-    for index in range(3):
-        columns = slice(index * D, (index + 1) * D)
-        part = dot(normed, w_ref[:, columns]) + dot(mixed, b_ref[:, columns])
-        if index == 0:
-            qt_ref[...] = (part * QUERY_SCALE).astype(BF16).T
-        else:
-            low = part.astype(BF16)
-            natural, turned = ((k_ref, kt_ref), (v_ref, vt_ref))[index - 1]
-            natural[...] = low
-            turned[...] = low.T
-
-    if link is not None:
-
-        @pl.when(step == pl.num_programs(0) - 1)
-        def _():
-            phases[4]()
-            shards_ref[...] = landing[...]
-
-
-def project(x, gain, w_qkv, ar_qkv, b_qkv, shard, axes, sizes, span):
-    length = x.shape[0]
-    devices = sizes[0] * sizes[1]
-    link = None if devices == 1 else (axes, sizes, span)
-    groups = max(devices // 8, 1)
-    landing = (max(span[1] - span[0], 1), 8, *shard.shape)
-    if link is None:
-        landing = (1, 8, 16, LANES)
-    tile = pl.BlockSpec((ROWS, D), lambda i: (i, 0))
-    turned = pl.BlockSpec((D, ROWS), lambda i: (0, i))
-    natural_shape = jax.ShapeDtypeStruct((length, D), BF16)
-    turned_shape = jax.ShapeDtypeStruct((D, length), BF16)
-    return pl.pallas_call(
-        functools.partial(project_kernel, link),
-        grid=(length // ROWS,),
-        in_specs=[
-            whole(shard.shape),
-            tile,
-            whole((1, D)),
-            whole(w_qkv.shape),
-            whole(ar_qkv.shape),
-            whole(b_qkv.shape),
-        ],
-        out_specs=[
-            turned,
-            tile,
-            turned,
-            tile,
-            turned,
-            pl.BlockSpec((6 * COLS, ROWS), lambda i: (0, i)),
-            whole(landing),
-        ],
-        out_shape=[
-            turned_shape,
-            natural_shape,
-            turned_shape,
-            natural_shape,
-            turned_shape,
-            jax.ShapeDtypeStruct((6 * COLS, length), F32),
-            jax.ShapeDtypeStruct(landing, BF16),
-        ],
-        scratch_shapes=[pltpu.VMEM(landing, BF16), *gather_semaphores(groups)],
-        compiler_params=params()
-        if link is None
-        else params(collective_id=1, has_side_effects=True),
-        name="project",
-    )(shard, x, gain, w_qkv, ar_qkv, b_qkv)
 
 
 def bias_table(offset_row, length):
@@ -322,7 +217,6 @@
 
 
 def attend_back_kernel(
-    link,
     length_ref,
     off_ref,
     qt_ref,
@@ -332,41 +226,15 @@
     ot_ref,
     gt_ref,
     lse_ref,
-    parts_ref,
-    sums_ref,
     dq_ref,
     dk_ref,
     dv_ref,
-    rest_ref,
-    roots_ref,
     table,
     key_more,
     weights_all,
     grads_all,
-    *scratch,
 ):
     length = k_ref.shape[0]
-    step = pl.program_id(0)
-
-    def finish_sums(total):
-        roots_ref[...] = jnp.sqrt(total / (total[:, 4:5] * D))
-
-    if link is None:
-        finish_sums(sums_ref[...])
-    else:
-        axes, sizes, span = link
-        *boxes, total, near_out, near_in, send, receive = scratch
-        ring = Ring(axes, sizes, send, receive)
-        phases = reduce_phases(
-            ring, span, parts_ref, (*boxes, total), sums_ref, (near_out, near_in)
-        )
-        for turn, phase in enumerate(phases[:4]):
-            pl.when(step == turn)(phase)
-
-        @pl.when(step == pl.num_programs(0) - 1)
-        def _():
-            phases[4](finish_sums)
-            rest_ref[...] = total[...]
 
     @pl.when(pl.program_id(0) == 0)
     def _():
@@ -413,30 +281,13 @@
     dq_ref[...] = jnp.concatenate(grad_query_parts, axis=0).T.astype(BF16)
 
 
-def attend_back(
-    length_valid, offsets, qt, k, kt, v, ot, gt, lse, parts, sums, axes, sizes, span
-):
+def attend_back(length_valid, offsets, qt, k, kt, v, ot, gt, lse):
     length = k.shape[0]
-    devices = sizes[0] * sizes[1]
-    link = None if devices == 1 else (axes, sizes, span)
-    rows = parts.shape[-2]
-    rest_rows = rows if link else 8
-    more = []
-    if link:
-        groups = devices // 8
-        copies = 10 + 2 * groups
-        more = reduce_scratch(groups, span[1] - span[0], rows) + [
-            pltpu.VMEM((rows, LANES), F32),
-            pltpu.VMEM((4, *sums.shape), F32),
-            pltpu.VMEM((3 + groups, *sums.shape), F32),
-            pltpu.SemaphoreType.DMA((copies,)),
-            pltpu.SemaphoreType.DMA((copies,)),
-        ]
     turned = pl.BlockSpec((LANES, length), lambda p: (p, 0))
     natural = pl.BlockSpec((length, LANES), lambda p: (0, p))
     natural_shape = jax.ShapeDtypeStruct((length, D), BF16)
     return pl.pallas_call(
-        functools.partial(attend_back_kernel, link),
+        attend_back_kernel,
         grid=(HEADS // 2,),
         in_specs=[
             pl.BlockSpec(memory_space=pltpu.SMEM),
@@ -448,25 +299,18 @@
             turned,
             turned,
             pl.BlockSpec((1, 2, length), lambda p: (p, 0, 0)),
-            whole(parts.shape) if link else pl.BlockSpec(memory_space=pl.ANY),
-            whole(sums.shape),
         ],
-        out_specs=[natural] * 3 + [whole((rest_rows, LANES)), whole(sums.shape)],
-        out_shape=[natural_shape] * 3
-        + [
-            jax.ShapeDtypeStruct((rest_rows, LANES), F32),
-            jax.ShapeDtypeStruct(sums.shape, F32),
-        ],
+        out_specs=[natural] * 3,
+        out_shape=[natural_shape] * 3,
         scratch_shapes=[
             pltpu.VMEM((2, LANES, 2 * length), F32),
             pltpu.VMEM((2, length, LANES), BF16),
             pltpu.VMEM((length, length), BF16),
             pltpu.VMEM((length, length), BF16),
-        ]
-        + more,
-        compiler_params=params(collective_id=2, has_side_effects=True) if link else params(),
+        ],
+        compiler_params=params(),
         name="attend_back",
-    )(length_valid, offsets, qt, k, kt, v, ot, gt, lse, parts, sums)
+    )(length_valid, offsets, qt, k, kt, v, ot, gt, lse)
 
 
 def middle_kernel(
@@ -877,11 +721,7 @@
         out_ref[:, lanes] = jnp.concatenate(parts, axis=0).astype(BF16)
 
 
-def unpack_first_kernel(
-    count, shards_ref, buckets_ref, table_ref, ar_ref, b_ref, off_ref, flat, down, router
-):
-    for index in range(-(-FIRST_COUNT // count)):
-        align_in(flat, shards_ref[index].astype(F32), index * count)
+def unpack_first(flat, ar_ref, b_ref, down, router):
     starts = piece_rows()
     narrow_to_rows(flat, D, [(starts[k][0], COLS, k * COLS) for k in range(3)], down)
     narrow_to_rows(flat, D, [(starts[k][2], EXPERTS, k * EXPERTS) for k in range(3)], router)
@@ -893,47 +733,13 @@
         ar_ref[:, half * LANES : (half + 1) * LANES] = packed.astype(BF16)
     for index in range(3):
         unpack_ups(flat, starts[index][1], D, index * COLS, b_ref, index * D)
-    buckets = buckets_ref[...]
-    hits = jnp.where(row_iota((table_ref.shape[0], buckets.shape[1])) == buckets, LOG2E, 0.0)
-    off_ref[...] = lax.dot_general(
-        table_ref[...],
-        hits,
-        (((0,), (0,)), ((), ())),
-        preferred_element_type=F32,
-        precision=lax.Precision.HIGHEST,
-    )
 
 
 def flat_rows(count):
     return PARAM_ROWS + shard_rows(count) + 20
 
 
-def unpack_first(shards, buckets, rel_table, count):
-    return pl.pallas_call(
-        functools.partial(unpack_first_kernel, count),
-        in_specs=[pl.BlockSpec(memory_space=pltpu.VMEM)] * 3,
-        out_specs=[pl.BlockSpec(memory_space=pltpu.VMEM)] * 3,
-        out_shape=[
-            jax.ShapeDtypeStruct((D, 2 * LANES), BF16),
-            jax.ShapeDtypeStruct((LANES, 3 * D), BF16),
-            jax.ShapeDtypeStruct((HEADS, buckets.shape[1]), F32),
-        ],
-        scratch_shapes=[
-            pltpu.VMEM((flat_rows(count), LANES), F32),
-            pltpu.VMEM((D, LANES), F32),
-            pltpu.VMEM((D, LANES), F32),
-        ],
-        compiler_params=params(),
-        name="unpack_first",
-    )(shards, buckets, rel_table)
-
-
-def unpack_rest_kernel(count, first_ref, rest_ref, *refs):
-    *outs, flat, work = refs
-    split = first_ref.shape[0]
-    for index in range(FIRST_COUNT // count, PARAM_ROWS * LANES // count):
-        shard = first_ref[index] if index < split else rest_ref[index - split]
-        align_in(flat, shard.astype(F32), index * count)
+def unpack_rest(flat, outs, work):
     starts = piece_rows()
     matrix = (keep_matrix() + spread_matrix(EXPERTS, COLS, COLS)).astype(BF16)
     for index in range(3, 6):
@@ -945,22 +751,6 @@
         unpack_ups(flat, base_b, fan_out, 0, b_ref, 0)
 
 
-def unpack_rest(first, rest, count):
-    shapes = [shape for fan_in, fan_out in FANS[3:] for shape in ((fan_in, LANES), (LANES, fan_out))]
-    return pl.pallas_call(
-        functools.partial(unpack_rest_kernel, count),
-        in_specs=[pl.BlockSpec(memory_space=pltpu.VMEM)] * 2,
-        out_specs=[pl.BlockSpec(memory_space=pltpu.VMEM)] * len(shapes),
-        out_shape=[jax.ShapeDtypeStruct(shape, BF16) for shape in shapes],
-        scratch_shapes=[
-            pltpu.VMEM((flat_rows(count), LANES), F32),
-            pltpu.VMEM((FF, LANES), F32),
-        ],
-        compiler_params=params(),
-        name="unpack_rest",
-    )(first, rest)
-
-
 def split_dot(value, matrix):
     high = value.astype(BF16)
     return dot(high, matrix) + dot((value - high.astype(F32)).astype(BF16), matrix)
@@ -980,44 +770,19 @@
         flat[pl.ds(base + k, COLS, stride=width), :] = grad_ref[first : first + COLS, lanes]
 
 
-def assemble_rest_kernel(count, split, *refs):
-    *ins, shards_ref, more_ref, flat, work = refs
+def assemble_rest(flat, grads, work):
     starts = piece_rows()
     matrix = (keep_matrix() + first_of_four(EXPERTS, COLS, COLS)).astype(BF16)
     for index in range(3, 6):
         base_a, base_b, base_r = starts[index]
         fan_in, fan_out = FANS[index]
-        dar_ref, db_ref = ins[2 * index - 6], ins[2 * index - 5]
+        dar_ref, db_ref = grads[2 * index - 6], grads[2 * index - 5]
         work[:fan_in] = split_dot(pad_rows(dar_ref[...], LANES).T, matrix)
         rows_to_narrow(work, fan_in, [(base_a, COLS, 0), (base_r, EXPERTS, COLS)], flat)
         assemble_ups(flat, base_b, fan_out, 0, db_ref, 0)
-    for index in range(shards_ref.shape[0]):
-        shards_ref[index] = align_out(flat, shards_ref.shape[1], (split + index) * count)
-    begin = FIRST_COUNT // LANES
-    more_ref[...] = flat[begin : begin + more_ref.shape[0]]
-
-
-def assemble_rest(grads, devices, split, count):
-    rows = shard_rows(count)
-    more = (split * count - FIRST_COUNT) // (8 * LANES) * 8 + 16
-    return pl.pallas_call(
-        functools.partial(assemble_rest_kernel, count, split),
-        in_specs=[pl.BlockSpec(memory_space=pltpu.VMEM)] * len(grads),
-        out_specs=[pl.BlockSpec(memory_space=pltpu.VMEM)] * 2,
-        out_shape=[
-            jax.ShapeDtypeStruct((max(devices - split, 1), rows, LANES), F32),
-            jax.ShapeDtypeStruct((more, LANES), F32),
-        ],
-        scratch_shapes=[
-            pltpu.VMEM((flat_rows(count), LANES), F32),
-            pltpu.VMEM((FF, LANES), F32),
-        ],
-        compiler_params=params(),
-        name="assemble_rest",
-    )(*grads)
-
-
-def assemble_first_kernel(count, dar_ref, db_ref, more_ref, shards_ref, flat, down, router):
+
+
+def assemble_first(flat, dar_ref, db_ref, down, router):
     starts = piece_rows()
     down[...] = dar_ref[:LANES].T
     rows_to_narrow(down, D, [(starts[k][0], COLS, k * COLS) for k in range(3)], flat)
@@ -1027,27 +792,6 @@
     rows_to_narrow(router, D, [(starts[k][2], EXPERTS, k * EXPERTS) for k in range(3)], flat)
     for index in range(3):
         assemble_ups(flat, starts[index][1], D, index * COLS, db_ref, index * D)
-    begin = FIRST_COUNT // LANES
-    flat[begin : begin + more_ref.shape[0]] = more_ref[...]
-    for index in range(shards_ref.shape[0]):
-        shards_ref[index] = align_out(flat, shards_ref.shape[1], index * count)
-
-
-def assemble_first(dar, db, more, split, count):
-    rows = shard_rows(count)
-    return pl.pallas_call(
-        functools.partial(assemble_first_kernel, count),
-        in_specs=[pl.BlockSpec(memory_space=pltpu.VMEM)] * 3,
-        out_specs=pl.BlockSpec(memory_space=pltpu.VMEM),
-        out_shape=jax.ShapeDtypeStruct((split, rows, LANES), F32),
-        scratch_shapes=[
-            pltpu.VMEM((flat_rows(count), LANES), F32),
-            pltpu.VMEM((D, LANES), F32),
-            pltpu.VMEM((D, LANES), F32),
-        ],
-        compiler_params=params(),
-        name="assemble_first",
-    )(dar, db, more)
 
 
 MESH = pl.DeviceIdType.MESH
@@ -1116,7 +860,7 @@
         )
 
 
-def gather_phases(ring, span, shard_ref, out_ref, local):
+def gather_phases(ring, span, shard_ref, out_ref, local, greets):
     begin, end = span
     base = ring.groups
     inside = (ring.group >= begin) & (ring.group < end)
@@ -1159,7 +903,8 @@
         )
 
     def phase0():
-        ring.greet()
+        if greets:
+            ring.greet()
 
         @pl.when(inside)
         def _():
@@ -1209,25 +954,177 @@
     ]
 
 
-def gather_kernel(axes, sizes, span, shard_ref, out_ref, send, receive, local):
-    for phase in gather_phases(Ring(axes, sizes, send, receive), span, shard_ref, out_ref, local):
-        phase()
-
-
-def gather(shard, axes, sizes, span):
+def start_kernel(
+    link,
+    count,
+    shard_ref,
+    buckets_ref,
+    table_ref,
+    gain_ref,
+    x_hbm,
+    w_hbm,
+    *refs,
+):
+    hbm_outs, off_ref, ar_ref, b_ref = refs[:6], refs[6], refs[7], refs[8]
+    rest_refs = refs[9:15]
+    x_ref, w_ref, normed, dense = refs[15:19]
+    outs = refs[19:25]
+    qt_ref, k_ref, kt_ref, v_ref, vt_ref, zg_ref = outs
+    flat, down, router, work, loaded, stored, *more = refs[25:]
+    loads = [
+        pltpu.make_async_copy(x_hbm, x_ref, loaded.at[0]),
+        pltpu.make_async_copy(w_hbm, w_ref, loaded.at[1]),
+    ]
+    stores = [
+        pltpu.make_async_copy(source, target, stored.at[index])
+        for index, (source, target) in enumerate(zip(outs, hbm_outs))
+    ]
+    for load in loads:
+        load.start()
+    if link is None:
+        first = [lambda: None] * 5
+        rest = first
+
+        def shard_of(index):
+            return shard_ref[...]
+    else:
+        axes, sizes, spans = link
+        land_a, land_b, *sems = more
+        first = gather_phases(
+            Ring(axes, sizes, *sems[:2]), spans[0], shard_ref, land_a, sems[2], True
+        )
+        rest = gather_phases(
+            Ring(axes, sizes, *sems[3:5]), spans[1], shard_ref, land_b, sems[5], False
+        )
+
+        def shard_of(index):
+            group, low = divmod(index, 8)
+            begin = spans[1][0]
+            return land_a[group, low] if group < begin else land_b[group - begin, low]
+
+    def rows_of(index):
+        return pl.ds(pl.multiple_of(index * ROWS, ROWS), ROWS)
+
+    def dense_tile(index, _):
+        rows = rows_of(index)
+        values = x_ref[rows].astype(F32)
+        low = (values * rms_inverse(values) * gain_ref[...]).astype(BF16)
+        normed[rows] = low
+        dense[rows] = dot(low, w_ref[...])
+        return 0
+
+    def project_tile(index, _):
+        rows = rows_of(index)
+        packed = dot(normed[rows], ar_ref[...]).T
+        lowrank = packed[: 3 * COLS]
+        gates = jnp.concatenate(
+            [gates_of(packed[place : place + COLS]) for place in range(3 * COLS, 6 * COLS, COLS)],
+            axis=0,
+        )
+        zg_ref[: 3 * COLS, rows] = lowrank
+        zg_ref[3 * COLS :, rows] = gates
+        mixed = pad_rows(lowrank * gates, LANES).astype(BF16).T
+        for part in range(3):
+            columns = slice(part * D, (part + 1) * D)
+            value = dense[rows, columns] + dot(mixed, b_ref[:, columns])
+            if part == 0:
+                qt_ref[:, rows] = (value * QUERY_SCALE).astype(BF16).T
+            else:
+                low = value.astype(BF16)
+                natural, turned = ((k_ref, kt_ref), (v_ref, vt_ref))[part - 1]
+                natural[rows] = low
+                turned[:, rows] = low.T
+        return 0
+
+    tiles = x_ref.shape[0] // ROWS
+    first[0]()
+    rest[0]()
+    for load in loads:
+        load.wait()
+    lax.fori_loop(0, tiles // 2, dense_tile, 0)
+    first[1]()
+    rest[1]()
+    lax.fori_loop(tiles // 2, tiles, dense_tile, 0)
+    buckets = buckets_ref[...]
+    hits = jnp.where(row_iota((table_ref.shape[0], buckets.shape[1])) == buckets, LOG2E, 0.0)
+    off_ref[...] = lax.dot_general(
+        table_ref[...],
+        hits,
+        (((0,), (0,)), ((), ())),
+        preferred_element_type=F32,
+        precision=lax.Precision.HIGHEST,
+    )
+    for step in range(2, 5):
+        first[step]()
+        if step < 4:
+            rest[step]()
+
+    for index in range(-(-FIRST_COUNT // count)):
+        align_in(flat, shard_of(index).astype(F32), index * count)
+    unpack_first(flat, ar_ref, b_ref, down, router)
+    lax.fori_loop(0, tiles, project_tile, 0)
+    for store in stores:
+        store.start()
+    rest[4]()
+    for index in range(FIRST_COUNT // count, PARAM_ROWS * LANES // count):
+        align_in(flat, shard_of(index).astype(F32), index * count)
+    unpack_rest(flat, rest_refs, work)
+    for store in stores:
+        store.wait()
+
+
+def start(x, gain, w_qkv, shard, buckets, rel_table, count, axes, sizes, spans):
+    length = x.shape[0]
     groups = sizes[0] * sizes[1] // 8
+    link = (axes, sizes, spans) if groups else None
+    rest_shapes = [
+        shape for fan_in, fan_out in FANS[3:] for shape in ((fan_in, LANES), (LANES, fan_out))
+    ]
+    wide = [
+        ((D, length), BF16),
+        ((length, D), BF16),
+        ((D, length), BF16),
+        ((length, D), BF16),
+        ((D, length), BF16),
+        ((6 * COLS, length), F32),
+    ]
+    small = [
+        ((HEADS, buckets.shape[1]), F32),
+        ((D, 2 * LANES), BF16),
+        ((LANES, 3 * D), BF16),
+    ] + [(shape, BF16) for shape in rest_shapes]
+    scratch = [
+        pltpu.VMEM(x.shape, BF16),
+        pltpu.VMEM(w_qkv.shape, BF16),
+        pltpu.VMEM(x.shape, BF16),
+        pltpu.VMEM((length, 3 * D), F32),
+    ]
+    scratch += [pltpu.VMEM(*member) for member in wide]
+    scratch += [
+        pltpu.VMEM((flat_rows(count), LANES), F32),
+        pltpu.VMEM((D, LANES), F32),
+        pltpu.VMEM((D, LANES), F32),
+        pltpu.VMEM((FF, LANES), F32),
+        pltpu.SemaphoreType.DMA((2,)),
+        pltpu.SemaphoreType.DMA((len(wide),)),
+    ]
+    if link:
+        scratch += [pltpu.VMEM((end - begin, 8, *shard.shape), BF16) for begin, end in spans]
+        scratch += gather_semaphores(groups) * 2
+    vmem = pl.BlockSpec(memory_space=pltpu.VMEM)
+    anywhere = pl.BlockSpec(memory_space=pl.ANY)
     return pl.pallas_call(
-        functools.partial(gather_kernel, axes, sizes, span),
-        in_specs=[pl.BlockSpec(memory_space=pltpu.VMEM)],
-        out_specs=pl.BlockSpec(memory_space=pltpu.VMEM),
-        out_shape=jax.ShapeDtypeStruct((span[1] - span[0], 8, *shard.shape), shard.dtype),
-        scratch_shapes=gather_semaphores(groups),
-        compiler_params=params(collective_id=0, has_side_effects=True),
-        name="gather",
-    )(shard)
-
-
-def reduce_phases(ring, span, parts_ref, boxes, sums_ref=None, sum_boxes=None):
+        functools.partial(start_kernel, link, count),
+        in_specs=[vmem] * 4 + [anywhere] * 2,
+        out_specs=[anywhere] * len(wide) + [vmem] * len(small),
+        out_shape=[jax.ShapeDtypeStruct(*member) for member in wide + small],
+        scratch_shapes=scratch,
+        compiler_params=params(collective_id=0, has_side_effects=True) if link else params(),
+        name="start",
+    )(shard, buckets, rel_table, gain, x, w_qkv)
+
+
+def reduce_phases(ring, span, parts_ref, boxes, greets, sums_ref=None, sum_boxes=None):
     begin, end = span
     outbox, inbox, half, own, far_out, far_in, out_ref = boxes
     groups = ring.groups
@@ -1288,7 +1185,8 @@
             push_sums(slot).start()
 
     def phase0():
-        ring.greet()
+        if greets:
+            ring.greet()
         if sum_boxes is not None:
             start_sums(0, sums_ref[...])
         for slot, part in enumerate(core_parts):
@@ -1377,40 +1275,88 @@
     ]
 
 
-def reduce_kernel(axes, sizes, span, parts_ref, rest_ref, out_ref, *scratch):
-    *boxes, total, send, receive = scratch
-    ring = Ring(axes, sizes, send, receive)
-    for phase in reduce_phases(ring, span, parts_ref, (*boxes, total)):
-        phase()
-    first = (ring.group >= span[0]) & (ring.group < span[1])
-
-    @pl.when(first)
+def finish_kernel(link, count, dar_ref, db_ref, *refs):
+    grads, sums_ref = refs[:6], refs[6]
+    out_ref, roots_ref, flat, down, router, work, *more = refs[7:]
+
+    def finish_sums(total):
+        roots_ref[...] = jnp.sqrt(total / (total[:, 4:5] * D))
+
+    assemble_rest(flat, grads, work)
+    if link is None:
+        assemble_first(flat, dar_ref, db_ref, down, router)
+        out_ref[...] = align_out(flat, out_ref.shape[0], 0)
+        finish_sums(sums_ref[...])
+        return
+    axes, sizes, spans = link
+    parts_a, parts_b, near_out, near_in, *more = more
+    boxes_a, boxes_b, sems = more[:7], more[7:14], more[14:]
+    rows = out_ref.shape[0]
+    split = spans[1][0]
+
+    def align(parts, span):
+        for group in range(*span):
+            for low in range(8):
+                parts[group - span[0], low] = align_out(flat, rows, (8 * group + low) * count)
+
+    ring = Ring(axes, sizes, sems[0], sems[1])
+    rest = reduce_phases(ring, spans[1], parts_b, boxes_b, True, sums_ref, (near_out, near_in))
+    first = reduce_phases(
+        Ring(axes, sizes, sems[2], sems[3]), spans[0], parts_a, boxes_a, False
+    )
+    align(parts_b, spans[1])
+    rest[0]()
+    assemble_first(flat, dar_ref, db_ref, down, router)
+    align(parts_a, spans[0])
+    first[0]()
+    for step in range(1, 4):
+        rest[step]()
+        first[step]()
+    rest[4](finish_sums)
+    first[4]()
+
+    @pl.when(ring.group < split)
     def _():
-        out_ref[...] = total[...]
-
-    @pl.when(jnp.logical_not(first))
+        out_ref[...] = boxes_a[6][...]
+
+    @pl.when(ring.group >= split)
     def _():
-        out_ref[...] = rest_ref[...]
-
-
-def reduce_scatter(parts, rest, axes, sizes, span):
-    count, _, rows, lanes = parts.shape
+        out_ref[...] = boxes_b[6][...]
+
+
+def finish(dar, db, grads, sums, count, axes, sizes, spans):
+    rows = shard_rows(count)
     groups = sizes[0] * sizes[1] // 8
-    copies = 7 + groups
+    link = (axes, sizes, spans) if groups else None
+    scratch = [
+        pltpu.VMEM((flat_rows(count), LANES), F32),
+        pltpu.VMEM((D, LANES), F32),
+        pltpu.VMEM((D, LANES), F32),
+        pltpu.VMEM((FF, LANES), F32),
+    ]
+    if link:
+        widths = [end - begin for begin, end in spans]
+        scratch += [pltpu.VMEM((width, 8, rows, LANES), F32) for width in widths]
+        scratch += [
+            pltpu.VMEM((4, *sums.shape), F32),
+            pltpu.VMEM((3 + groups, *sums.shape), F32),
+        ]
+        for width in widths:
+            scratch += reduce_scratch(groups, width, rows) + [pltpu.VMEM((rows, LANES), F32)]
+        scratch += [pltpu.SemaphoreType.DMA((10 + 2 * groups,))] * 4
+    vmem = pl.BlockSpec(memory_space=pltpu.VMEM)
     return pl.pallas_call(
-        functools.partial(reduce_kernel, axes, sizes, span),
-        in_specs=[pl.BlockSpec(memory_space=pltpu.VMEM)] * 2,
-        out_specs=pl.BlockSpec(memory_space=pltpu.VMEM),
-        out_shape=jax.ShapeDtypeStruct((rows, lanes), F32),
-        scratch_shapes=reduce_scratch(groups, count, rows)
-        + [
-            pltpu.VMEM((rows, lanes), F32),
-            pltpu.SemaphoreType.DMA((copies,)),
-            pltpu.SemaphoreType.DMA((copies,)),
+        functools.partial(finish_kernel, link, count),
+        in_specs=[vmem] * (3 + len(grads)),
+        out_specs=[vmem] * 2,
+        out_shape=[
+            jax.ShapeDtypeStruct((rows, LANES), F32),
+            jax.ShapeDtypeStruct(sums.shape, F32),
         ],
-        compiler_params=params(collective_id=3, has_side_effects=True),
-        name="reduce_scatter",
-    )(parts, rest)
+        scratch_shapes=scratch,
+        compiler_params=params(collective_id=1, has_side_effects=True) if link else params(),
+        name="finish",
+    )(dar, db, *grads, sums)
 
 
 def per_device(
@@ -1440,39 +1386,21 @@
     shard = jnp.pad(adapters, (0, rows * LANES - count)).reshape(rows, LANES)
     groups = devices // 8
     split_groups = min(-(-FIRST_COUNT // (8 * count)), max(groups - 1, 1))
-    split = min(8 * split_groups, devices)
-    first_span, rest_span = (0, split_groups), (split_groups, groups)
-    if devices == 1:
-        first = shard[None]
-    else:
-        first = gather(shard, axes, sizes, first_span).reshape(split, rows, LANES)
+    spans = ((0, split_groups), (split_groups, groups))
     reversed_buckets = jnp.pad(buckets[::-1], (0, 1)).reshape(1, 2 * length)
-    ar_qkv, b_qkv, offsets = unpack_first(first, reversed_buckets, rel_table, count)
-    qt, k, kt, v, vt, zg, rest = project(
-        x, gain_first, w_qkv, ar_qkv, b_qkv, shard, axes, sizes, rest_span
+    qt, k, kt, v, vt, zg, offsets, ar_qkv, b_qkv, *packed = start(
+        x, gain_first, w_qkv, shard, reversed_buckets, rel_table, count, axes, sizes, spans
     )
-    rest = rest.reshape(-1, *rest.shape[2:])
     ot, lse = attend(lengths, offsets, qt, k, vt)
-    packed = unpack_rest(first, rest, count)
     block_out, dmid, gt, sums, *grads = middle_part(
         lengths, ot, x, cot, gain_second, w_out, w_in, w_down, packed
     )
-    parts, more = assemble_rest(grads, devices, split, count)
-    if devices > 1:
-        parts = parts.reshape(groups - split_groups, 8, rows, LANES)
-    dq, dk, dv, rest_sum, roots = attend_back(
-        lengths, offsets, qt, k, kt, v, ot, gt, lse, parts, sums, axes, sizes, rest_span
-    )
+    dq, dk, dv = attend_back(lengths, offsets, qt, k, kt, v, ot, gt, lse)
     tokens_grad, dar_qkv, db_qkv = project_back(
         x, gain_first, w_qkv, ar_qkv, b_qkv, zg, dq, dk, dv, dmid
     )
 
-    parts = assemble_first(dar_qkv, db_qkv, more, split, count)
-    if devices == 1:
-        mine = parts[0]
-    else:
-        parts = parts.reshape(split_groups, 8, rows, LANES)
-        mine = reduce_scatter(parts, rest_sum, axes, sizes, first_span)
+    mine, roots = finish(dar_qkv, db_qkv, grads, sums, count, axes, sizes, spans)
     grad_shard = mine.reshape(-1)[:count]
     root_squares = roots[0, :4]
     return (

time: 212 us -> 187 us (0.88)
  Pallas kernels: 200 us -> 175 us
    pallas_call x8 -> x3, Pallas kernels: 115 us -> 90.3 us  [the longest x1 35 us: attend_back(): pl.pallas_call(attend_back_kernel, grid=(HEADS // 2,), in_specs=[pl.Block...]
where the time goes in v2:
time: 187 us; the launch traced here: 186 us
  Pallas kernels  175 us (94%)
  local copies, waits for them, and re-layouts  9.48 us (5%)
    pallas_call x1, Pallas kernels, middle_part(): pl.pallas_call(middle_kernel, grid=(length // MIDDLE_ROWS,), in_specs=[pl...  52.6 us
    pallas_call x1, Pallas kernels, attend_back(): pl.pallas_call(attend_back_kernel, grid=(HEADS // 2,), in_specs=[pl.Block...  35 us
    pallas_call x1, Pallas kernels, start(): pl.pallas_call(functools.partial(start_kernel, link, count), in_specs=[vm...  31.2 us
    pallas_call x1, Pallas kernels, finish(): pl.pallas_call(functools.partial(finish_kernel, link, count), in_specs=[v...  24.2 us
    pallas_call x1, Pallas kernels, attend(): pl.pallas_call(attend_kernel, grid=(HEADS // 2,), in_specs=[pl.BlockSpec(...  19.7 us
    pallas_call x1, Pallas kernels, project_back(): pl.pallas_call(project_back_kernel, grid=(length // ROWS,), in_specs=[til...  12.6 us

profile of v2, /device:TPU:0, one launch (start us, length us, event | category | flops | bytes accessed | tf_op | source)
XLA Modules:
  0.0 186.1 jit_solution(13335935621176291696)
XLA Ops:
  1.3 1.3 reshape.37.gain_ref
  2.5 1.3 reshape.40.gain_ref
  3.8 0.8 reverse
  4.6 0.1 slice.10
  4.7 0.6 pad.9
  5.3 1.4 copy.16.table_ref
  6.7 1.4 pad_bitcast_fusion.shard_ref
  8.0 31.2 %start.1 = (bf16[768,1024]{1,0:T(8,128)(2,1)}, bf16[1024,768]{1,0:T(8,128)(2,1)}, bf16[768,1024]{1,0:T(8,128)(2,1)}, bf16[1024,768]{1,0:T(8,128)(2,1)}, bf16[768...) custom-call(bf16[160,128]{1,0:T(8,128)(2,1)} %pad_bitcast_fusion.sha, ...), custom_call_target="tpu_custom_call" | custom-call | tf_op jit(solution)/shard_map/start/pallas_call | solution.py:1116
  39.2 19.7 %attend.1 = (bf16[768,1024]{1,0:T(8,128)(2,1)}, f32[6,2,1024]{2,1,0:T(2,128)}) custom-call(s32[1]{0:T(128)S(6)} %copy.17.length_ref, f32[12,2048]{1,0:T(8,128)} %get-tuple-element.39.off_ref, bf16[768,1024]{1,0:T(8,128)(2,1)} %get-tuple-element.40.qt_ref, bf16[1024,768]{1,0:T(8,128)(2,1)} %get-tuple-element.41.k_ref, bf16[768,1024]{1,0:T(8,128)(2,1)} %get-tuple-element.42.vt_ref), custom_call_target="tpu_custom_call" | custom-call | tf_op jit(solution)/shard_map/attend/pallas_call | solution.py:195
  58.9 52.6 %middle_part.1 = (bf16[1024,768]{1,0:T(8,128)(2,1)}, f32[1024,768]{1,0:T(8,128)}, bf16[768,1024]{1,0:T(8,128)(2,1)}, f32[8,128]{1,0:T(8,128)}, f32[80,768]{1,0:T...) custom-call(s32[1]{0:T(128)S(6)} %copy.17.length_ref, ...), custom_call_target="tpu_custom_call" | custom-call | tf_op jit(solution)/shard_map/middle_part/pallas_call | solution.py:498
  111.6 35.0 %attend_back.1 = (bf16[1024,768]{1,0:T(8,128)(2,1)}, bf16[1024,768]{1,0:T(8,128)(2,1)}, bf16[1024,768]{1,0:T(8,128)(2,1)}) custom-call(s32[1]{0:T(128)S(6)} %copy.17.length_ref, f32[12,2048]{1,0:T(8,128)} %get-tuple-element.39.off_ref, bf16[768,1024]{1,0:T(8,128)(2,1)} %get-tuple-element.40.qt_ref, bf16[1024,768]{1,0:T(8,128)(2,1)} %get-tuple-element.41.k_ref, ...), custom_call_target="tpu_custom_call" | custom-call | tf_op jit(solution)/shard_map/attend_back/pallas_call | solution.py:289
  146.5 12.6 %project_back.1 = (f32[1024,768]{1,0:T(8,128)}, f32[256,768]{1,0:T(8,128)}, f32[128,2304]{1,0:T(8,128)}) custom-call(bf16[1024,768]{1,0:T(8,128)(2,1)} %bitcast.13, f32[1,768]{1,0:T(1,128)} %reshape.37.gain_ref, bf16[768,2304]{1,0:T(8,128)(2,1)} %w_ref.1, bf16[768,256]{1,0:T(8,128)(2,1)} %get-tuple-element.51.ar_ref, ...), custom_call_target="tpu_custom_call" | custom-call | tf_op jit(solution)/shard_map/project_back/pallas_call | solution.py:578
  159.1 24.2 %finish.1 = (f32[160,128]{1,0:T(8,128)}, f32[8,128]{1,0:T(8,128)}) custom-call(f32[256,768]{1,0:T(8,128)} %get-tuple-element.63.dar_ref, f32[128,2304]{1,0:T(8,128)} %get-tuple-element.64.db_ref, f32[80,768]{1,0:T(8,128)} %get-tuple-element.65.refs_0_, f32[48,768]{1,0:T(8,128)} %get-tuple-element.66.refs_1_, f32[80,768]{1,0:T(8,128)} %get-tuple-element.67.refs_2_, ...), custom_call_target="tpu_custom_call" | custom-call | tf_op jit(solution)/shard_map/finish/pallas_call | solution.py:1348
  183.3 1.5 slice.8
  184.9 1.2 slice_bitcast_fusion
